TPU v7x, 256 devices: a whole 4x4x8 slice. The times are simulated.
256 devices in a mesh: img: 32 (over z_lo, y, core), txt: 8 (over z_hi, x).
Axes of the slice: x: 4, y: 4, z: 8 (z_hi: 2, z_lo: 4; z = z_hi * 4 + z_lo), core: 2. Of those that a mesh axis runs over, the one named last changes fastest.
Arguments:
- text_states: bfloat16 [512, 77, 1280], P(('img', 'txt')), may hold values from -6 to 6
- text_length: int32 [512], P(('img', 'txt')), may hold values from 1 to 77, as said below
- sample_count: int32 [256], P(('img', 'txt')), may hold values from 1 to 2, as said below
- mlp_gain: float32 [1280], replicated, may hold values from 0.1 to 1.9
- up_weight: bfloat16 [1280, 5120], P(None, 'txt'), may hold values from -0.15625 to 0.15625
- down_weight: bfloat16 [5120, 1280], P('txt'), may hold values from -0.078125 to 0.078125
- final_gain: float32 [1280], replicated, may hold values from 0.1 to 1.9
- text_proj: bfloat16 [1280, 1280], replicated, may hold values from -0.15625 to 0.15625
- image_pooled: bfloat16 [512, 1664], P(('img', 'txt')), may hold values from -6 to 6
- image_gain: float32 [1664], replicated, may hold values from 0.1 to 1.9
- image_proj: bfloat16 [1664, 1280], replicated, may hold values from -0.15625 to 0.15625
- logit_scale: float32 [], replicated, may hold values from 20 to 100
Outputs:
- image_proj_grad: float32 [1664, 1280], P('txt', 'img')
- up_grad: float32 [1280, 5120], P('img', 'txt')
- down_grad: float32 [5120, 1280], P('txt', 'img')
Inputs may be any that keep to these rules, and one draw needn't show every extreme that they name: Text b has text_length[b] real tokens; the longest text has 77. Slot k of device d holds a real image and text pair exactly when k < sample_count[d]; some device has all 2 slots filled.
All inputs are finite; a program needn't handle non-finite values.
Results may differ from a plain program's by a relative error of at most 0.035.
Values may be sent and summed in bfloat16 or wider, within the bound.
No kernel may reach another device: no remote copies, remote signals or barrier semaphores. Data moves between devices by JAX's collectives and lax.ppermute only.
A program may use at most 128 MiB of HBM per device.

v0:
```python
import jax
import jax.numpy as jnp
from jax import lax
from jax.experimental import pallas as pl
from jax.experimental.pallas import tpu as pltpu
from jax.sharding import PartitionSpec as P

EPSILON = 1e-05
ROOT_HALF = 0.7071067811865476
INV_ROOT_TAU = 0.3989422804014327
BF = jnp.bfloat16
F32 = jnp.float32
PAD = 80


def centre(values):
    return values - jnp.mean(values, axis=-1, keepdims=True)


def inv_std_of(centred):
    return lax.rsqrt(jnp.mean(centred * centred, axis=-1, keepdims=True) + EPSILON)


def unit_rows(raw):
    inv_norm = lax.rsqrt(jnp.sum(raw * raw, axis=-1, keepdims=True) + 1e-06)
    return (raw * inv_norm, inv_norm)


def unit_back(grad_unit, direction, inv_norm):
    return inv_norm * (
        grad_unit - direction * jnp.sum(direction * grad_unit, axis=-1, keepdims=True)
    )


VMEM_LIMIT = 40 * 1024 * 1024
OVER_ROWS = (((0,), (0,)), ((), ()))
OVER_COLS = (((1,), (1,)), ((), ()))


def call(kernel, outs, *operands, scratch=(), smem=0, anywhere=0, flops=0):
    size = sum(v.size * v.dtype.itemsize for v in operands) + sum(
        v.size * v.dtype.itemsize for v in outs
    )
    specs = [pl.BlockSpec(memory_space=pltpu.SMEM)] * smem
    specs += [pl.BlockSpec(memory_space=pl.ANY)] * anywhere
    specs += [pl.BlockSpec(memory_space=pltpu.VMEM)] * (len(operands) - smem - anywhere)
    return pl.pallas_call(
        kernel,
        out_shape=outs,
        in_specs=specs,
        out_specs=[pl.BlockSpec(memory_space=pltpu.VMEM)] * len(outs),
        scratch_shapes=list(scratch),
        cost_estimate=pl.CostEstimate(flops=flops, bytes_accessed=size, transcendentals=0),
        compiler_params=pltpu.CompilerParams(vmem_limit_bytes=VMEM_LIMIT),
    )(*operands)


def shape(rows, cols, dtype):
    return jax.ShapeDtypeStruct((rows, cols), dtype)


def padded(states_ref, slot, scratch):
    length = states_ref.shape[1]
    scratch[PAD - 8 :, :] = jnp.zeros((8, scratch.shape[1]), F32)
    scratch[:length, :] = states_ref[slot].astype(F32)
    return scratch[...]


def norm_kernel(count_ref, length_ref, states_ref, image_ref, gain_ref, out_ref, scratch):
    length = states_ref.shape[1]
    width = out_ref.shape[1]
    rest = image_ref.shape[1] - width
    lane = lax.broadcasted_iota(jnp.int32, (1, 128), 1)
    image = image_ref[...].astype(F32)
    for slot in range(states_ref.shape[0]):
        centred = centre(padded(states_ref, slot, scratch))
        scratch[...] = centred * inv_std_of(centred) * gain_ref[...]
        valid = (slot < count_ref[0]).astype(F32)
        flags = jnp.where(lane == 0, valid, length_ref[slot].astype(F32))
        scratch[length : length + 1, :] = image[slot : slot + 1, :width]
        scratch[length + 1 : length + 2, :rest] = image[slot : slot + 1, width:]
        scratch[length + 1 : length + 2, rest : rest + 128] = jnp.where(lane < 2, flags, 0.0)
        out_ref[slot * PAD : (slot + 1) * PAD, :] = scratch[...].astype(BF)


def forward_kernel(
    own_ref, left_ref, right_ref, far_ref, up_ref, down_ref,
    normed_ref, act_ref, slope_ref, image_ref, o_own, o_left, o_right, o_far_a, o_far_b,
):
    rows = own_ref.shape[0]
    image = []
    for k, ref in enumerate((own_ref, left_ref, right_ref, far_ref)):
        normed_ref[k * rows : (k + 1) * rows, :] = ref[...]
        for end in range(PAD, rows + 1, PAD):
            last = ref[end - 16 : end, :].astype(F32)
            image.append(jnp.concatenate([last[13:14, :], last[14:15, :512]], axis=1))
    image_ref[...] = jnp.concatenate(image, axis=0).astype(BF)
    for part in range(2):
        span = slice(2 * part * rows, 2 * (part + 1) * rows)
        preact = jnp.dot(normed_ref[span, :], up_ref[...], preferred_element_type=F32)
        cdf = 0.5 * (1.0 + lax.erf(preact * ROOT_HALF))
        act_ref[span, :] = (preact * cdf).astype(BF)
        slope = cdf + preact * INV_ROOT_TAU * jnp.exp(-0.5 * preact * preact)
        slope_ref[span, :] = slope.astype(BF)
        out = jnp.dot(act_ref[span, :], down_ref[...], preferred_element_type=F32)
        if part == 0:
            o_own[...] = out[:rows]
            o_left[...] = out[rows:]
        else:
            o_right[...] = out[:rows]
            o_far_a[...] = out[rows : rows + rows // 2].astype(BF)
            o_far_b[...] = out[rows + rows // 2 :].astype(BF)


def relay_kernel(left_ref, right_ref, got_a_ref, got_b_ref, o_left, o_right):
    half = got_a_ref.shape[0]
    o_right[:half, :] = (right_ref[:half, :] + got_a_ref[...].astype(F32)).astype(BF)
    o_right[half:, :] = right_ref[half:, :].astype(BF)
    o_left[:half, :] = left_ref[:half, :].astype(BF)
    o_left[half:, :] = (left_ref[half:, :] + got_b_ref[...].astype(F32)).astype(BF)


def away_kernel(own_ref, left_ref, right_ref, out_ref):
    total = own_ref[...] + left_ref[...].astype(F32) + right_ref[...].astype(F32)
    out_ref[...] = total.astype(BF)


def final_kernel(
    length_ref, states_ref, own_ref, left_ref, right_ref, away_ref, gain_ref,
    pooled_ref, centred_ref, half_a_ref, half_b_ref, scratch,
):
    pooled = []
    for slot in range(states_ref.shape[0]):
        span = slice(slot * PAD, (slot + 1) * PAD)
        total = own_ref[span, :] + left_ref[span, :].astype(F32) + right_ref[span, :].astype(F32)
        total = total + away_ref[span, :].astype(F32)
        centred = centre(padded(states_ref, slot, scratch) + total)
        centred_ref[span, :] = centred.astype(BF)
        (half_a_ref, half_b_ref)[slot][...] = centred.astype(BF)
        count = length_ref[slot]
        kept = (lax.broadcasted_iota(jnp.int32, (PAD, 1), 0) < count).astype(F32)
        weight = kept * inv_std_of(centred) / count.astype(F32)
        pooled.append(jnp.sum(centred * weight, axis=0, keepdims=True) * gain_ref[...])
    pooled_ref[...] = jnp.concatenate(pooled, axis=0).astype(BF)


def split_core(core, rows, part, send_ref, keep_ref):
    run = 40
    for j in range(rows.shape[0] // (4 * run)):
        first = rows[j * 4 * run : j * 4 * run + run]
        second = rows[j * 4 * run + run : j * 4 * run + 2 * run]
        third = rows[j * 4 * run + 2 * run : j * 4 * run + 3 * run]
        fourth = rows[j * 4 * run + 3 * run : j * 4 * run + 4 * run]
        even = jnp.concatenate([first, third], axis=0)
        odd = jnp.concatenate([second, fourth], axis=0)
        base = part * rows.shape[0] // 2 + j * 2 * run
        span = slice(base, base + 2 * run)
        send_ref[span, :] = jnp.where(core == 0, odd, even).astype(BF)
        keep_ref[span, :] = jnp.where(core == 0, even, odd).astype(BF)


def hidden_kernel(
    core_ref, length_ref, h0, h1, h2, h3, h4, h5, h6, h7, pulled_ref, act_a_ref, act_b_ref,
    grad_ref, send_ref, keep_ref, hidden_ref, arrived,
):
    rows = h0.shape[0]
    pieces = [
        pltpu.make_async_copy(ref, hidden_ref.at[pl.ds(k * rows, rows)], arrived.at[k])
        for k, ref in enumerate((h0, h1, h2, h3, h4, h5, h6, h7))
    ]
    for piece in pieces:
        piece.start()
    for piece in pieces:
        piece.wait()

    def sample(index, carry):
        span = pl.ds(pl.multiple_of(index * PAD, PAD), PAD)
        centred = hidden_ref[span, :].astype(F32)
        inv = inv_std_of(centred)
        hat = centred * inv
        pulled = pulled_ref[pl.ds(index, 1), :]
        along = jnp.mean(pulled * hat, axis=-1, keepdims=True)
        count = length_ref[index]
        kept = (lax.broadcasted_iota(jnp.int32, (PAD, 1), 0) < count).astype(F32)
        weight = kept * inv / count.astype(F32)
        grad = weight * (pulled - jnp.mean(pulled, axis=-1, keepdims=True) - hat * along)
        grad_ref[span, :] = grad.astype(BF)
        return carry

    lax.fori_loop(0, grad_ref.shape[0] // PAD, sample, 0)
    tokens = act_a_ref.shape[0]
    for part in range(2):
        cols = slice(part * 640, (part + 1) * 640)
        rows = lax.dot_general(
            grad_ref[:tokens, cols], act_a_ref[...], OVER_ROWS, preferred_element_type=F32
        ) + lax.dot_general(
            grad_ref[tokens:, cols], act_b_ref[...], OVER_ROWS, preferred_element_type=F32
        )
        split_core(core_ref[0], rows, part, send_ref, keep_ref)


def weights_kernel(
    core_ref, grad_ref, down_ref, slope_a_ref, slope_b_ref, normed_a_ref, normed_b_ref,
    send_ref, keep_ref, scratch,
):
    tokens = slope_a_ref.shape[0]
    for part, slope_ref in enumerate((slope_a_ref, slope_b_ref)):
        span = slice(part * tokens, (part + 1) * tokens)
        back = lax.dot_general(
            grad_ref[span, :], down_ref[...], OVER_COLS, preferred_element_type=F32
        )
        scratch[span, :] = (back * slope_ref[...].astype(F32)).astype(BF)
    for part in range(2):
        cols = slice(part * 640, (part + 1) * 640)
        rows = lax.dot_general(
            normed_a_ref[:, cols], scratch[:tokens, :], OVER_ROWS, preferred_element_type=F32
        ) + lax.dot_general(
            normed_b_ref[:, cols], scratch[tokens:, :], OVER_ROWS, preferred_element_type=F32
        )
        split_core(core_ref[0], rows, part, send_ref, keep_ref)


def spread_y_kernel(y_ref, keep_ref, got_ref, own_ref, s1_ref, s2_ref, s3_ref, scratch):
    scratch[...] = keep_ref[...].astype(F32) + got_ref[...].astype(F32)
    for shift, ref in ((0, own_ref), (1, s1_ref), (3, s2_ref), (2, s3_ref)):
        place = lax.rem(y_ref[0] + shift, 4) * 40
        for pair in range(2):
            runs = [
                scratch[pl.ds(pl.multiple_of((2 * pair + k) * 160 + place, 8), 40), :]
                for k in range(2)
            ]
            ref[pair * 80 : (pair + 1) * 80, :] = jnp.concatenate(runs, axis=0).astype(ref.dtype)


def spread_z_kernel(z_ref, keep_ref, r1_ref, r2_ref, r3_ref, own_ref, s1_ref, s2_ref, s3_ref, scratch):
    scratch[...] = (
        keep_ref[...]
        + r1_ref[...].astype(F32)
        + r2_ref[...].astype(F32)
        + r3_ref[...].astype(F32)
    )
    for shift, ref in ((0, own_ref), (1, s1_ref), (3, s2_ref), (2, s3_ref)):
        place = lax.rem(z_ref[0] + shift, 4) * 40
        ref[...] = scratch[pl.ds(pl.multiple_of(place, 8), 40), :].astype(ref.dtype)


def move_txt(value, z_hi=0, x=0):
    pairs = [
        (a * 4 + b, ((a + z_hi) % 2) * 4 + (b + x) % 4) for a in range(2) for b in range(4)
    ]
    return lax.ppermute(value, "txt", pairs)


def move_img(value, z_lo=0, y=0, core=0):
    pairs = [
        (a * 8 + b * 2 + c, ((a + z_lo) % 4) * 8 + ((b + y) % 4) * 2 + (c + core) % 2)
        for a in range(4)
        for b in range(4)
        for c in range(2)
    ]
    return lax.ppermute(value, "img", pairs)


def nought(*events):
    return sum(event[0, 0].astype(F32) for event in events) * 0.0


def joined(*rows):
    return lax.optimization_barrier(jnp.concatenate(rows, axis=0))


def ring_txt(rows):
    return rows, move_txt(rows, x=1), move_txt(rows, x=-1), move_txt(rows, x=2)


def ring_z(rows):
    return rows, move_img(rows, z_lo=1), move_img(rows, z_lo=-1), move_img(rows, z_lo=2)


def ring_y(rows):
    return rows, move_img(rows, y=1), move_img(rows, y=-1), move_img(rows, y=2)


def gather_core(rows):
    return jnp.concatenate([rows, move_img(rows, core=1)], axis=0)


def ring_x(piece, way):
    left, right = move_txt(piece, x=1), move_txt(piece, x=-1)
    return piece, left, right, move_txt(left if way > 0 else right, x=way)


def ring_x_back(terms, held=None):
    own, left, right, far_a, far_b = terms
    got_a = move_txt(far_a, x=1)
    got_b = move_txt(far_b, x=-1)
    if held is not None:
        got_a, got_b, held = lax.optimization_barrier((got_a, got_b, held))
    left, right = call(
        relay_kernel, (shape(left.shape[0], left.shape[1], BF),) * 2, left, right, got_a, got_b
    )
    return (own, move_txt(right, x=1), move_txt(left, x=-1)), held


def forward(pieces, up_weight, down_weight):
    rows = pieces[0].shape[0]
    tokens = 4 * rows
    width, units = up_weight.shape
    return call(
        forward_kernel,
        (
            shape(tokens, width, BF),
            shape(tokens, units, BF),
            shape(tokens, units, BF),
            shape(tokens // PAD, width + 512, BF),
        )
        + (shape(rows, width, F32),) * 3
        + (shape(rows // 2, width, BF),) * 2,
        *pieces,
        up_weight,
        down_weight,
        flops=4 * tokens * width * units,
    )


def sum_img_start(send, keep, y):
    got = move_img(send, core=1)
    cols = keep.shape[1]
    outs = (shape(160, cols, F32),) + (shape(160, cols, BF),) * 3
    own, s1, s2, s3 = call(
        spread_y_kernel, outs, y, keep, got, scratch=[pltpu.VMEM(keep.shape, F32)], smem=1
    )
    return own, s1, s2, s3


def sum_img_end(terms, z_lo):
    own, s1, s2, s3 = terms
    cols = own.shape[1]
    s3, s1, s2 = move_img(s3, y=2), move_img(s1, y=1), move_img(s2, y=-1)
    outs = (shape(40, cols, F32),) + (shape(40, cols, BF),) * 3
    own, s1, s2, s3 = call(
        spread_z_kernel, outs, z_lo, own, s1, s2, s3,
        scratch=[pltpu.VMEM((160, cols), F32)], smem=1,
    )
    s3, s1, s2 = move_img(s3, z_lo=2), move_img(s1, z_lo=1), move_img(s2, z_lo=-1)
    return own + s1.astype(F32) + s2.astype(F32) + s3.astype(F32)


def body(
    text_states,
    text_length,
    sample_count,
    mlp_gain,
    up_weight,
    down_weight,
    final_gain,
    text_proj,
    image_pooled,
    image_gain,
    image_proj,
    logit_scale,
):
    samples, length, width = text_states.shape
    image_width = image_pooled.shape[1]
    txt = lax.axis_index("txt")
    img = lax.axis_index("img")
    z_lo, y, core = img // 8, (img // 2) % 4, img % 2

    row_gain = mlp_gain.reshape(1, width)
    row_final = final_gain.reshape(1, width)

    rows = samples * PAD
    padding = pltpu.VMEM((PAD, width), F32)
    (normed_own,) = call(
        norm_kernel,
        (shape(rows, width, BF),),
        sample_count,
        text_length,
        text_states,
        image_pooled,
        row_gain,
        scratch=[padding],
        smem=2,
    )
    near = ring_x(normed_own, 1)
    normed_far = move_txt(normed_own, z_hi=1) + nought(near[2]).astype(BF)
    away = ring_x(normed_far, -1)
    normed_near, act_near, slope_near, image_near, *terms_near = forward(
        near, up_weight, down_weight
    )
    normed_away, act_away, slope_away, image_away, *terms_away = forward(
        away, up_weight, down_weight
    )
    image_rows = jnp.concatenate([image_near, image_away], axis=0)
    image_rows = jnp.concatenate(ring_z(image_rows), axis=0)
    terms_away, image_rows = ring_x_back(terms_away, image_rows)
    terms_near, _ = ring_x_back(terms_near)
    (away_sum,) = call(away_kernel, (shape(rows, width, BF),), *terms_away)
    from_away, image_rows = lax.optimization_barrier(
        (move_txt(away_sum, z_hi=1), jnp.concatenate(ring_y(image_rows), axis=0))
    )

    pooled, hidden, half_a, half_b = call(
        final_kernel,
        (shape(samples, width, BF), shape(rows, width, BF)) + (shape(PAD, width, BF),) * 2,
        text_length,
        text_states,
        *terms_near,
        from_away,
        row_final,
        scratch=[padding],
        smem=1,
    )
    def together(*values):
        return lax.optimization_barrier(values)

    def rows_of(pieces):
        return jnp.concatenate(pieces, axis=0)

    pooled, hidden, half_a, half_b, image_rows = together(
        pooled, hidden, half_a, half_b, image_rows
    )
    left, right = move_txt(hidden, x=1), move_txt(hidden, x=-1)
    pooled_x, left, right, half_a, half_b, image_all = together(
        rows_of(ring_txt(pooled)), left, right, move_txt(half_a, z_hi=1), half_b,
        gather_core(image_rows),
    )
    pooled_txt, far, hidden_far, left, right = together(
        rows_of((pooled_x, move_txt(pooled_x, z_hi=1))), move_txt(left, x=1),
        rows_of((half_a, move_txt(half_b, z_hi=1))), left, right,
    )
    hidden_near = (hidden, left, right, far)
    pooled_z, far_left, far_right, hidden_far = together(
        rows_of(ring_z(pooled_txt)),
        move_txt(hidden_far, x=1), move_txt(hidden_far, x=-1), hidden_far,
    )
    pooled_y, far_far, far_left, far_right, hidden_far = together(
        rows_of(ring_y(pooled_z)), move_txt(far_right, x=-1), far_left, far_right, hidden_far
    )
    hidden_away = (hidden_far, far_left, far_right, far_far)

    valid = image_all[:, image_width] > 0.5
    lengths = image_all[: 8 * samples, image_width + 1].astype(jnp.int32)
    image_centred = centre(image_all[:, :image_width].astype(F32))
    image_normed = (image_centred * inv_std_of(image_centred) * image_gain).astype(BF)
    image_raw = jnp.dot(image_normed, image_proj, preferred_element_type=F32)
    image_unit, image_inv = unit_rows(image_raw)
    image_send = image_unit.astype(BF)

    pooled_all = gather_core(pooled_y)

    group = 8 * samples
    text_raw = jnp.dot(pooled_all, text_proj, preferred_element_type=F32)
    text_unit, text_inv = unit_rows(text_raw)
    text_send = text_unit.astype(BF)
    scores = logit_scale * lax.dot_general(
        text_send, image_send, OVER_COLS, preferred_element_type=F32
    )
    batch = scores.shape[0]

    def masked_logsum(axis, mask):
        top = jnp.max(jnp.where(mask, scores, -1e30), axis=axis, keepdims=True)
        total = jnp.sum(jnp.exp(jnp.where(mask, scores - top, -1e30)), axis=axis, keepdims=True)
        return top + jnp.log(total)

    row_lse = masked_logsum(0, valid[:, None])
    col_lse = masked_logsum(1, valid[None, :])
    pair_mask = valid[:, None] & valid[None, :]
    row_prob = jnp.exp(jnp.where(pair_mask, scores - row_lse, -1e30))
    col_prob = jnp.exp(jnp.where(pair_mask, scores - col_lse, -1e30))
    same = jnp.arange(batch)[:, None] == jnp.arange(batch)[None, :]
    grad_scores = 0.5 * (row_prob + col_prob) - jnp.where(pair_mask & same, 1.0, 0.0)
    grad_high = lax.reduce_precision(grad_scores, 8, 7)
    grad_low = (grad_scores - grad_high).astype(BF)
    grad_high = grad_high.astype(BF)

    grad_text_unit = logit_scale * (
        jnp.dot(grad_high[:group], image_send, preferred_element_type=F32)
        + jnp.dot(grad_low[:group], image_send, preferred_element_type=F32)
    )
    grad_text_raw = unit_back(grad_text_unit, text_unit[:group], text_inv[:group]).astype(BF)
    grad_pooled = lax.dot_general(
        grad_text_raw, text_proj, OVER_COLS, preferred_element_type=F32
    )
    pulled = grad_pooled * final_gain
    core_at, y_at, z_at = (v.reshape(1).astype(jnp.int32) for v in (core, y, z_lo))
    units = act_near.shape[1]
    tokens = group * PAD
    sums = (shape(width // 2, units, BF),) * 2
    grad_hidden, down_send, down_keep = call(
        hidden_kernel,
        (shape(tokens, width, BF),) + sums,
        core_at,
        lengths,
        *hidden_near,
        *hidden_away,
        pulled,
        act_near,
        act_away,
        scratch=[pltpu.VMEM((tokens, width), BF), pltpu.SemaphoreType.DMA((8,))],
        smem=2,
        anywhere=8,
        flops=2 * tokens * width * units,
    )
    up_send, up_keep = call(
        weights_kernel,
        sums,
        core_at,
        grad_hidden,
        down_weight,
        slope_near,
        slope_away,
        normed_near,
        normed_away,
        scratch=[pltpu.VMEM((tokens, units), BF)],
        smem=1,
        flops=4 * tokens * width * units,
    )
    down_terms = sum_img_start(down_send, down_keep, y_at)
    up_terms = sum_img_start(up_send, up_keep, y_at)
    down_grad = sum_img_end(down_terms, z_at).T
    up_grad = sum_img_end(up_terms, z_at)

    grad_image_unit = logit_scale * (
        lax.dot_general(grad_high, text_send, OVER_ROWS, preferred_element_type=F32)
        + lax.dot_general(grad_low, text_send, OVER_ROWS, preferred_element_type=F32)
    )
    grad_image_raw = unit_back(grad_image_unit, image_unit, image_inv).astype(BF)
    columns = grad_image_raw.shape[1] // 32
    chosen = jnp.arange(grad_image_raw.shape[1])[:, None] == (
        img * columns + jnp.arange(columns)[None, :]
    )
    own_columns = jnp.dot(
        grad_image_raw, chosen.astype(BF), preferred_element_type=F32
    ).astype(BF)
    projected = lax.dot_general(image_normed, own_columns, OVER_ROWS, preferred_element_type=F32)
    rows = image_width // 8
    image_proj_grad = lax.dynamic_slice_in_dim(projected, txt * rows, rows, axis=0)
    return (image_proj_grad, up_grad, down_grad)


def solution(mesh):
    return jax.shard_map(
        body,
        mesh=mesh,
        in_specs=(
            P(("img", "txt"), None, None),
            P(("img", "txt")),
            P(("img", "txt")),
            P(),
            P(None, "txt"),
            P("txt", None),
            P(),
            P(),
            P(("img", "txt"), None),
            P(),
            P(),
            P(),
        ),
        out_specs=(P("txt", "img"), P("img", "txt"), P("txt", "img")),
        check_vma=False,
    )
```

profile of v0, /device:TPU:6, one launch (start us, length us, event | category | flops | bytes accessed | tf_op | source)
XLA Modules:
  0.0 258.3 jit_solution(7009111382310782307)
XLA Ops:
  6.4 7.2 %collective-permute-start.7 = (bf16[160,1280]{1,0:T(8,128)(2,1)S(1)}, bf16[160,1280]{1,0:T(8,128)(2,1)S(1)}, u32[]{:S(2)}, u32[]{:S(2)}) collective-permute-start(bf16[160,1280]{1,0:T(8,128)(2,1)S(1)} %shard_map.139.own_ref), channel_id=1, source_target_pairs={{0,4},{1,5},{2,6},{3,7},{4,0},{5,1},{6,2},{7,3},{8,12},{9,13},{10,... | collective-permute-start | bytes 1228808 | tf_op jit(solution)/shard_map/ppermute | solution.py:251
  13.6 2.4 collective-permute-start
  16.0 2.0 collective-permute-done.1.right_ref
  19.2 11.0 %collective-permute-done.7 = bf16[160,1280]{1,0:T(8,128)(2,1)S(1)} collective-permute-done((bf16[160,1280]{1,0:T(8,128)(2,1)S(1)}, bf16[160,1280]{1,0:T(8,128)(2,1)S(1)}, u32[]{:S(2)}, u32[]{:S(2)}) %collective-permute-start.7) | collective-permute-done | bytes 409632 | tf_op jit(solution)/shard_map/ppermute | solution.py:251
  30.8 2.7 %collective-permute-start.2 = (bf16[160,1280]{1,0:T(8,128)(2,1)S(1)}, bf16[160,1280]{1,0:T(8,128)(2,1)S(1)}, u32[]{:S(2)}, u32[]{:S(2)}) collective-permute-start(bf16[160,1280]{1,0:T(8,128)(2,1)S(1)} %collective-permute-done.left_ref), channel_id=1, source_target_pairs={{0,1},{1,2},{2,3},{3,0},{4,5},{5,6},{6,7},{7,4},{8,9},{9,10},{10,1... | collective-permute-start | bytes 1228808 | tf_op jit(solution)/shard_map/ppermute | solution.py:251
  34.7 8.8 %collective-permute-done.9.right_ref = bf16[160,1280]{1,0:T(8,128)(2,1)S(1)} collective-permute-done((bf16[160,1280]{1,0:T(8,128)(2,1)S(1)}, bf16[160,1280]{1,0:T(8,128)(2,1)S(1)}, u32[]{:S(2)}, u32[]{:S(2)}) %collective-permute-start.9) | collective-permute-done | bytes 409632 | tf_op jit(solution)/shard_map/ppermute | solution.py:251
  43.5 1.4 copy-done.14
  44.9 1.4 copy-done.16
  46.4 3.4 %shard_map.140 = (bf16[640,1280]{1,0:T(8,128)(2,1)S(1)}, bf16[640,640]{1,0:T(8,128)(2,1)S(1)}, bf16[640,640]{1,0:T(8,128)(2,1)S(1)}, bf16[8,1792]{1,0:T(8,128)(2...) custom-call(bf16[160,1280]{1,0:T(8,128)(2,1)S(1)} %shard_map.139.own, ...), custom_call_target="tpu_custom_call" | custom-call | flops 2097152000 | bytes 11087872 | tf_op jit(solution)/shard_map/pallas_call | solution.py:47
  51.0 1.6 collective-permute-done.10.far_ref
  52.7 3.4 %shard_map.142 = (bf16[640,1280]{1,0:T(8,128)(2,1)S(1)}, bf16[640,640]{1,0:T(8,128)(2,1)S(1)}, bf16[640,640]{1,0:T(8,128)(2,1)S(1)}, bf16[8,1792]{1,0:T(8,128)(2...) custom-call(bf16[160,1280]{1,0:T(8,128)(2,1)S(1)} %broadcast_add_fus, ...), custom_call_target="tpu_custom_call" | custom-call | flops 2097152000 | bytes 11087872 | tf_op jit(solution)/shard_map/pallas_call | solution.py:47
  56.1 2.2 collective-permute-start.13
  58.3 1.9 collective-permute-start.14
  60.3 1.8 collective-permute-start.15
  62.1 1.6 collective-permute-start.11
  64.1 1.7 collective-permute-done.15
  65.8 2.0 collective-permute-done.11.got_a_ref
  67.8 3.6 %collective-permute-done.12.got_b_ref = bf16[80,1280]{1,0:T(8,128)(2,1)S(1)} collective-permute-done((bf16[80,1280]{1,0:T(8,128)(2,1)S(1)}, bf16[80,1280]{1,0:T(8,128)(2,1)S(1)}, u32[]{:S(2)}, u32[]{:S(2)}) %collective-permute-start.12) | collective-permute-done | bytes 204832 | tf_op jit(solution)/shard_map/ppermute | solution.py:251
  71.6 2.0 collective-permute-start.17
  73.6 1.3 collective-permute-start.3
  75.6 3.2 %collective-permute-start.21 = (bf16[64,1792]{1,0:T(8,128)(2,1)S(1)}, bf16[64,1792]{1,0:T(8,128)(2,1)S(1)}, u32[]{:S(2)}, u32[]{:S(2)}) collective-permute-start(bf16[64,1792]{1,0:T(8,128)(2,1)S(1)} %constant_dynamic-update-slice_fusion.2), channel_id=1, source_target_pairs={{0,32},{8,40},{16,48},{24,56},{32,0},{40,8},{48,16},{56,24},{64,96... | collective-permute-start | bytes 688136 | tf_op jit(solution)/shard_map/ppermute | solution.py:261
  78.8 2.9 %collective-permute-done.3.got_a_ref = bf16[80,1280]{1,0:T(8,128)(2,1)S(1)} collective-permute-done((bf16[80,1280]{1,0:T(8,128)(2,1)S(1)}, bf16[80,1280]{1,0:T(8,128)(2,1)S(1)}, u32[]{:S(2)}, u32[]{:S(2)}) %collective-permute-start.3) | collective-permute-done | bytes 204832 | tf_op jit(solution)/shard_map/ppermute | solution.py:251
  81.8 3.0 %collective-permute-start.20 = (bf16[64,1792]{1,0:T(8,128)(2,1)S(1)}, bf16[64,1792]{1,0:T(8,128)(2,1)S(1)}, u32[]{:S(2)}, u32[]{:S(2)}) collective-permute-start(bf16[64,1792]{1,0:T(8,128)(2,1)S(1)} %constant_dynamic-update-slice_fusion.2), channel_id=1, source_target_pairs={{0,48},{8,56},{16,0},{24,8},{32,16},{40,24},{48,32},{56,40},{64,11... | collective-permute-start | bytes 688136 | tf_op jit(solution)/shard_map/ppermute | solution.py:261
  85.7 6.0 %collective-permute-start.18 = (bf16[160,1280]{1,0:T(8,128)(2,1)S(1)}, bf16[160,1280]{1,0:T(8,128)(2,1)S(1)}, u32[]{:S(2)}, u32[]{:S(2)}) collective-permute-start(bf16[160,1280]{1,0:T(8,128)(2,1)S(1)} %shard_map.144), channel_id=1, source_target_pairs={{0,4},{1,5},{2,6},{3,7},{4,0},{5,1},{6,2},{7,3},{8,12},{9,13},{10,... | collective-permute-start | bytes 1228808 | tf_op jit(solution)/shard_map/ppermute | solution.py:251
  92.4 1.3 collective-permute-start.6
  94.7 4.9 %collective-permute-done.18.away_ref = bf16[160,1280]{1,0:T(8,128)(2,1)S(1)} collective-permute-done((bf16[160,1280]{1,0:T(8,128)(2,1)S(1)}, bf16[160,1280]{1,0:T(8,128)(2,1)S(1)}, u32[]{:S(2)}, u32[]{:S(2)}) %collective-permute-start.18) | collective-permute-done | bytes 409632 | tf_op jit(solution)/shard_map/ppermute | solution.py:251
  99.6 2.0 collective-permute-done.6.right_ref
  104.2 12.6 %collective-permute-start.23 = (bf16[2,1280]{1,0:T(2,128)(2,1)S(1)}, bf16[2,1280]{1,0:T(2,128)(2,1)S(1)}, u32[]{:S(2)}, u32[]{:S(2)}) collective-permute-start(bf16[2,1280]{1,0:T(2,128)(2,1)S(1)} %get-tuple-element.105), channel_id=1, source_target_pairs={{0,3},{1,0},{2,1},{3,2},{4,7},{5,4},{6,5},{7,6},{8,11},{9,8},{10,9... | collective-permute-start | bytes 15368 | tf_op jit(solution)/shard_map/ppermute | solution.py:251
  118.4 1.5 collective-permute-start.25
  120.5 4.4 %collective-permute-start.27 = (bf16[80,1280]{1,0:T(8,128)(2,1)}, bf16[80,1280]{1,0:T(8,128)(2,1)S(1)}, u32[]{:S(2)}, u32[]{:S(2)}) collective-permute-start(bf16[80,1280]{1,0:T(8,128)(2,1)} %copy-done.22), channel_id=1, source_target_pairs={{0,4},{1,5},{2,6},{3,7},{4,0},{5,1},{6,2},{7,3},{8,12},{9,13},{10,... | collective-permute-start | bytes 614408 | tf_op jit(solution)/shard_map/ppermute | solution.py:251
  124.9 1.6 pad_maximum_fusion
  126.5 4.5 %collective-permute-done.27 = bf16[80,1280]{1,0:T(8,128)(2,1)S(1)} collective-permute-done((bf16[80,1280]{1,0:T(8,128)(2,1)}, bf16[80,1280]{1,0:T(8,128)(2,1)S(1)}, u32[]{:S(2)}, u32[]{:S(2)}) %collective-permute-start.27) | collective-permute-done | bytes 204832 | tf_op jit(solution)/shard_map/ppermute | solution.py:251
  132.9 4.4 %collective-permute-start.29 = (bf16[8,1280]{1,0:T(8,128)(2,1)S(1)}, bf16[8,1280]{1,0:T(8,128)(2,1)S(1)}, u32[]{:S(2)}, u32[]{:S(2)}) collective-permute-start(bf16[8,1280]{1,0:T(8,128)(2,1)S(1)} %pad_maximum_fusion.6), channel_id=1, source_target_pairs={{0,4},{1,5},{2,6},{3,7},{4,0},{5,1},{6,2},{7,3},{8,12},{9,13},{10,... | collective-permute-start | bytes 61448 | tf_op jit(solution)/shard_map/ppermute | solution.py:251
  137.4 1.4 collective-permute-start.30
  138.7 1.6 collective-permute-start.31
  140.7 8.1 %collective-permute-done.31 = bf16[80,1280]{1,0:T(8,128)(2,1)S(1)} collective-permute-done((bf16[80,1280]{1,0:T(8,128)(2,1)S(1)}, bf16[80,1280]{1,0:T(8,128)(2,1)S(1)}, u32[]{:S(2)}, u32[]{:S(2)}) %collective-permute-start.31) | collective-permute-done | bytes 204832 | tf_op jit(solution)/shard_map/ppermute | solution.py:251
  148.9 7.0 %collective-permute-start.34 = (bf16[16,1280]{1,0:T(8,128)(2,1)S(1)}, bf16[16,1280]{1,0:T(8,128)(2,1)S(1)}, u32[]{:S(2)}, u32[]{:S(2)}) collective-permute-start(bf16[16,1280]{1,0:T(8,128)(2,1)S(1)} %pad_maximum_fusion.5), channel_id=1, source_target_pairs={{0,128},{8,136},{16,144},{24,152},{32,160},{40,168},{48,176},{56,1... | collective-permute-start | bytes 122888 | tf_op jit(solution)/shard_map/ppermute | solution.py:261
  155.9 2.0 collective-permute-start.32
  157.9 1.8 collective-permute-start.35
  159.9 5.0 %multiply_reduce_fusion.2 = (f32[512]{0:T(512)S(1)}, f32[512,1280]{1,0:T(8,128)S(1)}) fusion(bf16[1664,1280]{1,0:T(8,128)(2,1)} %param.22, f32[1664]{0:T(1024)S(1)} %copy-done.45, f32[512]{0:T(512)S(1)} %add_rsqrt_fusion.2, f32[512]{0:T(512)S(1)} %broadcast_multiply_fusion.1, bf16[512,1792]{1,0:T(8,128)(2,1)S(1)} %pad_maximum_fusion), kind=kOutput, calls=%fused_computation.12 | convolution fusion | flops 2186608128 | bytes 8599552 | tf_op jit(solution)/shard_map/dot_general | solution.py:446
  164.9 1.9 collective-permute-done.35.h5
  166.9 3.1 %collective-permute-done.36.h6 = bf16[160,1280]{1,0:T(8,128)(2,1)S(1)} collective-permute-done((bf16[160,1280]{1,0:T(8,128)(2,1)S(1)}, bf16[160,1280]{1,0:T(8,128)(2,1)S(1)}, u32[]{:S(2)}, u32[]{:S(2)}) %collective-permute-start.36) | collective-permute-done | bytes 409632 | tf_op jit(solution)/shard_map/ppermute | solution.py:251
  170.5 2.9 %collective-permute-start.38 = (bf16[64,1280]{1,0:T(8,128)(2,1)S(1)}, bf16[64,1280]{1,0:T(8,128)(2,1)S(1)}, u32[]{:S(2)}, u32[]{:S(2)}) collective-permute-start(bf16[64,1280]{1,0:T(8,128)(2,1)S(1)} %pad_maximum_fusion.4), channel_id=1, source_target_pairs={{0,48},{8,56},{16,0},{24,8},{32,16},{40,24},{48,32},{56,40},{64,11... | collective-permute-start | bytes 491528 | tf_op jit(solution)/shard_map/ppermute | solution.py:261
  174.4 2.5 collective-permute-done.39
  176.9 2.4 collective-permute-done.38
  180.0 3.4 %collective-permute-done.40.h7 = bf16[160,1280]{1,0:T(8,128)(2,1)S(1)} collective-permute-done((bf16[160,1280]{1,0:T(8,128)(2,1)S(1)}, bf16[160,1280]{1,0:T(8,128)(2,1)S(1)}, u32[]{:S(2)}, u32[]{:S(2)}) %collective-permute-start.40) | collective-permute-done | bytes 409632 | tf_op jit(solution)/shard_map/ppermute | solution.py:251
  184.2 1.7 collective-permute-done.41
  185.9 2.0 multiply_reduce_fusion.1
  193.4 9.2 %shard_map.146 = (bf16[1280,1280]{1,0:T(8,128)(2,1)S(1)}, bf16[640,640]{1,0:T(8,128)(2,1)S(1)}, bf16[640,640]{1,0:T(8,128)(2,1)S(1)}) custom-call(s32[1]{0:T(128)} %bitcast.3.core_ref, s32[16]{0:T(128)S(1)} %convert_reduce_fusion.1.length_ref, bf16[160,1280]{1,0:T(8,128)(2,1)S(1)} %copy-done.21, bf16[160,1280]{1,0:T(8,128)(2,1)S(1)} %collective-permute-done.25.h1, ...), custom_call_target="tpu_custom_call" | custom-call | flops 2097152000 | bytes 9912388 | tf_op jit(solution)/shard_map/pallas_call | solution.py:47
  204.5 6.6 %shard_map.147 = (bf16[640,640]{1,0:T(8,128)(2,1)}, bf16[640,640]{1,0:T(8,128)(2,1)S(1)}) custom-call(s32[1]{0:T(128)} %bitcast.3.core_ref, bf16[1280,1280]{1,0:T(8,128)(2,1)S(1)} %get-tuple-element.132.grad_ref, bf16[640,1280]{1,0:T(8,128)(2,1)S(1)} %copy-done.18, bf16[640,640]{1,0:T(8,128)(2,1)S(1)} %copy-done.32, bf16[640,640]{1,0:T(8,128)(2,1)S(1)} %copy-done.34, ...), custom_call_target="tpu_custom_call" | custom-call | flops 4194304000 | bytes 11468804 | tf_op jit(solution)/shard_map/pallas_call | solution.py:47
  212.8 3.0 %fusion.29 = f32[512,1280]{1,0:T(8,128)S(1)} fusion(bf16[512,512]{1,0:T(8,128)(2,1)} %copy-done.42, f32[512,1280]{1,0:T(8,128)} %copy-done.35), kind=kOutput, calls=%fused_computation.80 | convolution fusion | flops 671744000 | bytes 5767168 | tf_op jit(solution)/shard_map/dot_general | solution.py:525
  215.8 2.3 shard_map.148
  218.2 2.0 collective-permute-start.43
  220.2 2.7 %multiply_reduce_fusion = (f32[512]{0:T(512)S(1)}, f32[512,1280]{1,0:T(8,128)}) fusion(f32[512,1280]{1,0:T(8,128)S(1)} %copy-done.39, f32[512]{0:T(512)S(1)} %add_rsqrt_fusion.1, f32[512,1280]{1,0:T(8,128)S(1)} %fusion.29, bf16[512,512]{1,0:T(8,128)(2,1)S(1)} %copy-done.41, f32[512,1280]{1,0:T(8,128)S(1)} %copy-done.36, f32[]{:T(128)S(6)} %copy.25), kind=kOutput, calls=%fused_computation.10 | convolution fusion | flops 675020288 | bytes 11014148 | tf_op jit(solution)/shard_map/dot_general | solution.py:526
  222.9 1.2 collective-permute-start.44
  228.1 2.1 collective-permute-start.51
  230.9 1.4 collective-permute-start.52
  232.3 5.2 %fusion.13 = f32[1664,40]{0,1:T(8,128)} fusion(f32[512,1280]{1,0:T(8,128)} %get-tuple-element.173, f32[512,1280]{1,0:T(8,128)} %copy-done.38, f32[512]{0:T(512)S(1)} %get-tuple-element.172, f32[512]{0:T(512)S(1)} %add_rsqrt_fusion.1, s32[40]{0:T(128)S(1)} %iota_add_fusion, f32[1664]{0:T(1024)S(1)} %copy-done.45, f32[512]{0:T(512)S(1)} %add_rsqrt_fusion.2, ...), kind=kOutput, calls=%fused_computation.31 | convolution fusion | flops 128194560 | bytes 7228064 | tf_op jit(solution)/shard_map/dot_general | solution.py:536
  241.0 2.4 collective-permute-start.47
  243.4 1.5 constant_dynamic-slice_fusion
  247.1 2.4 collective-permute-start.55
  249.5 2.1 collective-permute-start.54
  252.2 1.8 collective-permute-done.54
  254.0 3.4 %collective-permute-done.53 = bf16[40,640]{1,0:T(8,128)(2,1)S(1)} collective-permute-done((bf16[40,640]{1,0:T(8,128)(2,1)S(1)}, bf16[40,640]{1,0:T(8,128)(2,1)S(1)}, u32[]{:S(2)}, u32[]{:S(2)}) %collective-permute-start.53) | collective-permute-done | bytes 51232 | tf_op jit(solution)/shard_map/ppermute | solution.py:261
  (198 shorter events, 43.1 us)
Async XLA Ops:
  0.6 185.3 %copy-start = (bf16[1280,1280]{1,0:T(8,128)(2,1)S(1)}, bf16[1280,1280]{1,0:T(8,128)(2,1)}, u32[]{:S(2)}) copy-start(bf16[1280,1280]{1,0:T(8,128)(2,1)} %param.19) | copy-start | bytes 9830404
  5.5 12.5 %collective-permute-start.1 = (bf16[160,1280]{1,0:T(8,128)(2,1)S(1)}, bf16[160,1280]{1,0:T(8,128)(2,1)S(1)}, u32[]{:S(2)}, u32[]{:S(2)}) collective-permute-start(bf16[160,1280]{1,0:T(8,128)(2,1)S(1)} %shard_map.139.own_ref), channel_id=1, source_target_pairs={{0,3},{1,0},{2,1},{3,2},{4,7},{5,4},{6,5},{7,6},{8,11},{9,8},{10,9... | collective-permute-start | bytes 1228808 | tf_op jit(solution)/shard_map/ppermute | solution.py:251
  6.4 23.8 %collective-permute-start.7 = (bf16[160,1280]{1,0:T(8,128)(2,1)S(1)}, bf16[160,1280]{1,0:T(8,128)(2,1)S(1)}, u32[]{:S(2)}, u32[]{:S(2)}) collective-permute-start(bf16[160,1280]{1,0:T(8,128)(2,1)S(1)} %shard_map.139.own_ref), channel_id=1, source_target_pairs={{0,4},{1,5},{2,6},{3,7},{4,0},{5,1},{6,2},{7,3},{8,12},{9,13},{10,... | collective-permute-start | bytes 1228808 | tf_op jit(solution)/shard_map/ppermute | solution.py:251
  13.6 17.2 %collective-permute-start = (bf16[160,1280]{1,0:T(8,128)(2,1)S(1)}, bf16[160,1280]{1,0:T(8,128)(2,1)S(1)}, u32[]{:S(2)}, u32[]{:S(2)}) collective-permute-start(bf16[160,1280]{1,0:T(8,128)(2,1)S(1)} %shard_map.139.own_ref), channel_id=1, source_target_pairs={{0,1},{1,2},{2,3},{3,0},{4,5},{5,6},{6,7},{7,4},{8,9},{9,10},{10,1... | collective-permute-start | bytes 1228808 | tf_op jit(solution)/shard_map/ppermute | solution.py:251
  30.2 13.3 %collective-permute-start.9 = (bf16[160,1280]{1,0:T(8,128)(2,1)S(1)}, bf16[160,1280]{1,0:T(8,128)(2,1)S(1)}, u32[]{:S(2)}, u32[]{:S(2)}) collective-permute-start(bf16[160,1280]{1,0:T(8,128)(2,1)S(1)} %broadcast_add_fusion.own_ref), channel_id=1, source_target_pairs={{0,3},{1,0},{2,1},{3,2},{4,7},{5,4},{6,5},{7,6},{8,11},{9,8},{10,9... | collective-permute-start | bytes 1228808 | tf_op jit(solution)/shard_map/ppermute | solution.py:251
  30.8 12.7 %collective-permute-start.2 = (bf16[160,1280]{1,0:T(8,128)(2,1)S(1)}, bf16[160,1280]{1,0:T(8,128)(2,1)S(1)}, u32[]{:S(2)}, u32[]{:S(2)}) collective-permute-start(bf16[160,1280]{1,0:T(8,128)(2,1)S(1)} %collective-permute-done.left_ref), channel_id=1, source_target_pairs={{0,1},{1,2},{2,3},{3,0},{4,5},{5,6},{6,7},{7,4},{8,9},{9,10},{10,1... | collective-permute-start | bytes 1228808 | tf_op jit(solution)/shard_map/ppermute | solution.py:251
  33.5 17.5 %collective-permute-start.8 = (bf16[160,1280]{1,0:T(8,128)(2,1)S(1)}, bf16[160,1280]{1,0:T(8,128)(2,1)S(1)}, u32[]{:S(2)}, u32[]{:S(2)}) collective-permute-start(bf16[160,1280]{1,0:T(8,128)(2,1)S(1)} %broadcast_add_fusion.own_ref), channel_id=1, source_target_pairs={{0,1},{1,2},{2,3},{3,0},{4,5},{5,6},{6,7},{7,4},{8,9},{9,10},{10,1... | collective-permute-start | bytes 1228808 | tf_op jit(solution)/shard_map/ppermute | solution.py:251
  43.5 9.2 %collective-permute-start.10 = (bf16[160,1280]{1,0:T(8,128)(2,1)S(1)}, bf16[160,1280]{1,0:T(8,128)(2,1)S(1)}, u32[]{:S(2)}, u32[]{:S(2)}) collective-permute-start(bf16[160,1280]{1,0:T(8,128)(2,1)S(1)} %collective-permute-done.9.right_ref), channel_id=1, source_target_pairs={{0,3},{1,0},{2,1},{3,2},{4,7},{5,4},{6,5},{7,6},{8,11},{9,8},{10,9... | collective-permute-start | bytes 1228808 | tf_op jit(solution)/shard_map/ppermute | solution.py:251
  56.1 29.6 %copy-start.25 = (bf16[640,1280]{1,0:T(8,128)(2,1)}, bf16[640,1280]{1,0:T(8,128)(2,1)S(1)}, u32[]{:S(2)}) copy-start(bf16[640,1280]{1,0:T(8,128)(2,1)S(1)} %get-tuple-element.136.normed_b_ref) | copy-start | bytes 4915204
  56.1 29.6 %copy-start.29 = (bf16[640,640]{1,0:T(8,128)(2,1)}, bf16[640,640]{1,0:T(8,128)(2,1)S(1)}, u32[]{:S(2)}) copy-start(bf16[640,640]{1,0:T(8,128)(2,1)S(1)} %get-tuple-element.131.act_b_ref) | copy-start | bytes 2457604
  56.1 29.6 %copy-start.33 = (bf16[640,640]{1,0:T(8,128)(2,1)}, bf16[640,640]{1,0:T(8,128)(2,1)S(1)}, u32[]{:S(2)}) copy-start(bf16[640,640]{1,0:T(8,128)(2,1)S(1)} %get-tuple-element.134.slope_b_ref) | copy-start | bytes 2457604
  56.1 8.0 %collective-permute-start.13 = (bf16[16,1792]{1,0:T(8,128)(2,1)S(1)}, bf16[16,1792]{1,0:T(8,128)(2,1)S(1)}, u32[]{:S(2)}, u32[]{:S(2)}) collective-permute-start(bf16[16,1792]{1,0:T(8,128)(2,1)S(1)} %get-tuple-element.163), channel_id=1, source_target_pairs={{0,64},{8,72},{16,80},{24,88},{32,96},{40,104},{48,112},{56,120},{... | collective-permute-start | bytes 172040 | tf_op jit(solution)/shard_map/ppermute | solution.py:261
  58.3 5.8 %collective-permute-start.14 = (bf16[16,1792]{1,0:T(8,128)(2,1)S(1)}, bf16[16,1792]{1,0:T(8,128)(2,1)S(1)}, u32[]{:S(2)}, u32[]{:S(2)}) collective-permute-start(bf16[16,1792]{1,0:T(8,128)(2,1)S(1)} %get-tuple-element.163), channel_id=1, source_target_pairs={{0,192},{8,200},{16,208},{24,216},{32,224},{40,232},{48,240},{56,2... | collective-permute-start | bytes 172040 | tf_op jit(solution)/shard_map/ppermute | solution.py:261
  60.3 5.6 %collective-permute-start.15 = (bf16[16,1792]{1,0:T(8,128)(2,1)S(1)}, bf16[16,1792]{1,0:T(8,128)(2,1)S(1)}, u32[]{:S(2)}, u32[]{:S(2)}) collective-permute-start(bf16[16,1792]{1,0:T(8,128)(2,1)S(1)} %get-tuple-element.163), channel_id=1, source_target_pairs={{0,128},{8,136},{16,144},{24,152},{32,160},{40,168},{48,176},{56,1... | collective-permute-start | bytes 172040 | tf_op jit(solution)/shard_map/ppermute | solution.py:261
  62.1 5.8 %collective-permute-start.11 = (bf16[80,1280]{1,0:T(8,128)(2,1)S(1)}, bf16[80,1280]{1,0:T(8,128)(2,1)S(1)}, u32[]{:S(2)}, u32[]{:S(2)}) collective-permute-start(bf16[80,1280]{1,0:T(8,128)(2,1)S(1)} %get-tuple-element.90), channel_id=1, source_target_pairs={{0,1},{1,2},{2,3},{3,0},{4,5},{5,6},{6,7},{7,4},{8,9},{9,10},{10,1... | collective-permute-start | bytes 614408 | tf_op jit(solution)/shard_map/ppermute | solution.py:251
  63.7 7.7 %collective-permute-start.12 = (bf16[80,1280]{1,0:T(8,128)(2,1)S(1)}, bf16[80,1280]{1,0:T(8,128)(2,1)S(1)}, u32[]{:S(2)}, u32[]{:S(2)}) collective-permute-start(bf16[80,1280]{1,0:T(8,128)(2,1)S(1)} %get-tuple-element.91), channel_id=1, source_target_pairs={{0,3},{1,0},{2,1},{3,2},{4,7},{5,4},{6,5},{7,6},{8,11},{9,8},{10,9... | collective-permute-start | bytes 614408 | tf_op jit(solution)/shard_map/ppermute | solution.py:251
  71.4 22.3 %copy-start.43 = (f32[1280]{0:T(1024)S(1)}, f32[1280]{0:T(1024)}, u32[]{:S(2)}) copy-start(f32[1280]{0:T(1024)} %param.18) | copy-start | bytes 15364
  71.5 14.0 %collective-permute-start.16 = (bf16[160,1280]{1,0:T(8,128)(2,1)S(1)}, bf16[160,1280]{1,0:T(8,128)(2,1)S(1)}, u32[]{:S(2)}, u32[]{:S(2)}) collective-permute-start(bf16[160,1280]{1,0:T(8,128)(2,1)S(1)} %get-tuple-element.96), channel_id=1, source_target_pairs={{0,1},{1,2},{2,3},{3,0},{4,5},{5,6},{6,7},{7,4},{8,9},{9,10},{10,1... | collective-permute-start | bytes 1228808 | tf_op jit(solution)/shard_map/ppermute | solution.py:251
  71.6 13.9 %collective-permute-start.17 = (bf16[160,1280]{1,0:T(8,128)(2,1)S(1)}, bf16[160,1280]{1,0:T(8,128)(2,1)S(1)}, u32[]{:S(2)}, u32[]{:S(2)}) collective-permute-start(bf16[160,1280]{1,0:T(8,128)(2,1)S(1)} %get-tuple-element.97), channel_id=1, source_target_pairs={{0,3},{1,0},{2,1},{3,2},{4,7},{5,4},{6,5},{7,6},{8,11},{9,8},{10,9... | collective-permute-start | bytes 1228808 | tf_op jit(solution)/shard_map/ppermute | solution.py:251
  73.6 8.1 %collective-permute-start.3 = (bf16[80,1280]{1,0:T(8,128)(2,1)S(1)}, bf16[80,1280]{1,0:T(8,128)(2,1)S(1)}, u32[]{:S(2)}, u32[]{:S(2)}) collective-permute-start(bf16[80,1280]{1,0:T(8,128)(2,1)S(1)} %get-tuple-element.83), channel_id=1, source_target_pairs={{0,1},{1,2},{2,3},{3,0},{4,5},{5,6},{6,7},{7,4},{8,9},{9,10},{10,1... | collective-permute-start | bytes 614408 | tf_op jit(solution)/shard_map/ppermute | solution.py:251
  74.9 9.9 %collective-permute-start.4 = (bf16[80,1280]{1,0:T(8,128)(2,1)S(1)}, bf16[80,1280]{1,0:T(8,128)(2,1)S(1)}, u32[]{:S(2)}, u32[]{:S(2)}) collective-permute-start(bf16[80,1280]{1,0:T(8,128)(2,1)S(1)} %get-tuple-element.84), channel_id=1, source_target_pairs={{0,3},{1,0},{2,1},{3,2},{4,7},{5,4},{6,5},{7,6},{8,11},{9,8},{10,9... | collective-permute-start | bytes 614408 | tf_op jit(solution)/shard_map/ppermute | solution.py:251
  75.6 16.8 %collective-permute-start.21 = (bf16[64,1792]{1,0:T(8,128)(2,1)S(1)}, bf16[64,1792]{1,0:T(8,128)(2,1)S(1)}, u32[]{:S(2)}, u32[]{:S(2)}) collective-permute-start(bf16[64,1792]{1,0:T(8,128)(2,1)S(1)} %constant_dynamic-update-slice_fusion.2), channel_id=1, source_target_pairs={{0,32},{8,40},{16,48},{24,56},{32,0},{40,8},{48,16},{56,24},{64,96... | collective-permute-start | bytes 688136 | tf_op jit(solution)/shard_map/ppermute | solution.py:261
  81.8 12.0 %collective-permute-start.20 = (bf16[64,1792]{1,0:T(8,128)(2,1)S(1)}, bf16[64,1792]{1,0:T(8,128)(2,1)S(1)}, u32[]{:S(2)}, u32[]{:S(2)}) collective-permute-start(bf16[64,1792]{1,0:T(8,128)(2,1)S(1)} %constant_dynamic-update-slice_fusion.2), channel_id=1, source_target_pairs={{0,48},{8,56},{16,0},{24,8},{32,16},{40,24},{48,32},{56,40},{64,11... | collective-permute-start | bytes 688136 | tf_op jit(solution)/shard_map/ppermute | solution.py:261
  84.8 9.0 %collective-permute-start.19 = (bf16[64,1792]{1,0:T(8,128)(2,1)S(1)}, bf16[64,1792]{1,0:T(8,128)(2,1)S(1)}, u32[]{:S(2)}, u32[]{:S(2)}) collective-permute-start(bf16[64,1792]{1,0:T(8,128)(2,1)S(1)} %constant_dynamic-update-slice_fusion.2), channel_id=1, source_target_pairs={{0,16},{8,24},{16,32},{24,40},{32,48},{40,56},{48,0},{56,8},{64,80... | collective-permute-start | bytes 688136 | tf_op jit(solution)/shard_map/ppermute | solution.py:261
  85.7 13.9 %collective-permute-start.18 = (bf16[160,1280]{1,0:T(8,128)(2,1)S(1)}, bf16[160,1280]{1,0:T(8,128)(2,1)S(1)}, u32[]{:S(2)}, u32[]{:S(2)}) collective-permute-start(bf16[160,1280]{1,0:T(8,128)(2,1)S(1)} %shard_map.144), channel_id=1, source_target_pairs={{0,4},{1,5},{2,6},{3,7},{4,0},{5,1},{6,2},{7,3},{8,12},{9,13},{10,... | collective-permute-start | bytes 1228808 | tf_op jit(solution)/shard_map/ppermute | solution.py:251
  91.7 8.0 %collective-permute-start.5 = (bf16[160,1280]{1,0:T(8,128)(2,1)S(1)}, bf16[160,1280]{1,0:T(8,128)(2,1)S(1)}, u32[]{:S(2)}, u32[]{:S(2)}) collective-permute-start(bf16[160,1280]{1,0:T(8,128)(2,1)S(1)} %get-tuple-element.85), channel_id=1, source_target_pairs={{0,1},{1,2},{2,3},{3,0},{4,5},{5,6},{6,7},{7,4},{8,9},{9,10},{10,1... | collective-permute-start | bytes 1228808 | tf_op jit(solution)/shard_map/ppermute | solution.py:251
  92.4 9.2 %collective-permute-start.6 = (bf16[160,1280]{1,0:T(8,128)(2,1)S(1)}, bf16[160,1280]{1,0:T(8,128)(2,1)S(1)}, u32[]{:S(2)}, u32[]{:S(2)}) collective-permute-start(bf16[160,1280]{1,0:T(8,128)(2,1)S(1)} %get-tuple-element.86), channel_id=1, source_target_pairs={{0,3},{1,0},{2,1},{3,2},{4,7},{5,4},{6,5},{7,6},{8,11},{9,8},{10,9... | collective-permute-start | bytes 1228808 | tf_op jit(solution)/shard_map/ppermute | solution.py:251
  104.1 20.8 %collective-permute-start.28 = (bf16[256,1792]{1,0:T(8,128)(2,1)}, bf16[256,1792]{1,0:T(8,128)(2,1)}, u32[]{:S(2)}, u32[]{:S(2)}) collective-permute-start(bf16[256,1792]{1,0:T(8,128)(2,1)} %pad_maximum_fusion.1), channel_id=1, source_target_pairs={{0,8},{8,0},{16,24},{24,16},{32,40},{40,32},{48,56},{56,48},{64,72... | collective-permute-start | bytes 2752520 | tf_op jit(solution)/shard_map/ppermute | solution.py:261
  104.1 15.8 %collective-permute-start.24 = (bf16[2,1280]{1,0:T(2,128)(2,1)S(1)}, bf16[2,1280]{1,0:T(2,128)(2,1)S(1)}, u32[]{:S(2)}, u32[]{:S(2)}) collective-permute-start(bf16[2,1280]{1,0:T(2,128)(2,1)S(1)} %get-tuple-element.105), channel_id=1, source_target_pairs={{0,2},{1,3},{2,0},{3,1},{4,6},{5,7},{6,4},{7,5},{8,10},{9,11},{10,... | collective-permute-start | bytes 15368 | tf_op jit(solution)/shard_map/ppermute | solution.py:251
  104.2 16.3 %collective-permute-start.23 = (bf16[2,1280]{1,0:T(2,128)(2,1)S(1)}, bf16[2,1280]{1,0:T(2,128)(2,1)S(1)}, u32[]{:S(2)}, u32[]{:S(2)}) collective-permute-start(bf16[2,1280]{1,0:T(2,128)(2,1)S(1)} %get-tuple-element.105), channel_id=1, source_target_pairs={{0,3},{1,0},{2,1},{3,2},{4,7},{5,4},{6,5},{7,6},{8,11},{9,8},{10,9... | collective-permute-start | bytes 15368 | tf_op jit(solution)/shard_map/ppermute | solution.py:251
  116.8 8.0 %collective-permute-start.22 = (bf16[2,1280]{1,0:T(2,128)(2,1)S(1)}, bf16[2,1280]{1,0:T(2,128)(2,1)S(1)}, u32[]{:S(2)}, u32[]{:S(2)}) collective-permute-start(bf16[2,1280]{1,0:T(2,128)(2,1)S(1)} %get-tuple-element.105), channel_id=1, source_target_pairs={{0,1},{1,2},{2,3},{3,0},{4,5},{5,6},{6,7},{7,4},{8,9},{9,10},{10,1... | collective-permute-start | bytes 15368 | tf_op jit(solution)/shard_map/ppermute | solution.py:251
  118.4 12.6 %collective-permute-start.25 = (bf16[160,1280]{1,0:T(8,128)(2,1)}, bf16[160,1280]{1,0:T(8,128)(2,1)S(1)}, u32[]{:S(2)}, u32[]{:S(2)}) collective-permute-start(bf16[160,1280]{1,0:T(8,128)(2,1)} %copy-done.20), channel_id=1, source_target_pairs={{0,1},{1,2},{2,3},{3,0},{4,5},{5,6},{6,7},{7,4},{8,9},{9,10},{10,1... | collective-permute-start | bytes 1228808 | tf_op jit(solution)/shard_map/ppermute | solution.py:251
  119.9 12.2 %collective-permute-start.26 = (bf16[160,1280]{1,0:T(8,128)(2,1)}, bf16[160,1280]{1,0:T(8,128)(2,1)S(1)}, u32[]{:S(2)}, u32[]{:S(2)}) collective-permute-start(bf16[160,1280]{1,0:T(8,128)(2,1)} %copy-done.20), channel_id=1, source_target_pairs={{0,3},{1,0},{2,1},{3,2},{4,7},{5,4},{6,5},{7,6},{8,11},{9,8},{10,9... | collective-permute-start | bytes 1228808 | tf_op jit(solution)/shard_map/ppermute | solution.py:251
  120.5 10.5 %collective-permute-start.27 = (bf16[80,1280]{1,0:T(8,128)(2,1)}, bf16[80,1280]{1,0:T(8,128)(2,1)S(1)}, u32[]{:S(2)}, u32[]{:S(2)}) collective-permute-start(bf16[80,1280]{1,0:T(8,128)(2,1)} %copy-done.22), channel_id=1, source_target_pairs={{0,4},{1,5},{2,6},{3,7},{4,0},{5,1},{6,2},{7,3},{8,12},{9,13},{10,... | collective-permute-start | bytes 614408 | tf_op jit(solution)/shard_map/ppermute | solution.py:251
  126.5 57.3 %copy-start.37 = (bf16[512,1792]{1,0:T(8,128)(2,1)}, bf16[512,1792]{1,0:T(8,128)(2,1)S(1)}, u32[]{:S(2)}) copy-start(bf16[512,1792]{1,0:T(8,128)(2,1)S(1)} %pad_maximum_fusion) | copy-start | bytes 5505028
  126.5 33.4 %copy-start.45 = (f32[1664]{0:T(1024)S(1)}, f32[1664]{0:T(1024)}, u32[]{:S(2)}) copy-start(f32[1664]{0:T(1024)} %param.21) | copy-start | bytes 19972
  132.9 7.8 %collective-permute-start.29 = (bf16[8,1280]{1,0:T(8,128)(2,1)S(1)}, bf16[8,1280]{1,0:T(8,128)(2,1)S(1)}, u32[]{:S(2)}, u32[]{:S(2)}) collective-permute-start(bf16[8,1280]{1,0:T(8,128)(2,1)S(1)} %pad_maximum_fusion.6), channel_id=1, source_target_pairs={{0,4},{1,5},{2,6},{3,7},{4,0},{5,1},{6,2},{7,3},{8,12},{9,13},{10,... | collective-permute-start | bytes 61448 | tf_op jit(solution)/shard_map/ppermute | solution.py:251
  137.4 11.5 %collective-permute-start.30 = (bf16[160,1280]{1,0:T(8,128)(2,1)S(1)}, bf16[160,1280]{1,0:T(8,128)(2,1)S(1)}, u32[]{:S(2)}, u32[]{:S(2)}) collective-permute-start(bf16[160,1280]{1,0:T(8,128)(2,1)S(1)} %collective-permute-done.25.h1), channel_id=1, source_target_pairs={{0,1},{1,2},{2,3},{3,0},{4,5},{5,6},{6,7},{7,4},{8,9},{9,10},{10,1... | collective-permute-start | bytes 1228808 | tf_op jit(solution)/shard_map/ppermute | solution.py:251
  138.7 10.1 %collective-permute-start.31 = (bf16[80,1280]{1,0:T(8,128)(2,1)S(1)}, bf16[80,1280]{1,0:T(8,128)(2,1)S(1)}, u32[]{:S(2)}, u32[]{:S(2)}) collective-permute-start(bf16[80,1280]{1,0:T(8,128)(2,1)S(1)} %get-tuple-element.114), channel_id=1, source_target_pairs={{0,4},{1,5},{2,6},{3,7},{4,0},{5,1},{6,2},{7,3},{8,12},{9,13},{10,... | collective-permute-start | bytes 614408 | tf_op jit(solution)/shard_map/ppermute | solution.py:251
  148.9 16.0 %collective-permute-start.34 = (bf16[16,1280]{1,0:T(8,128)(2,1)S(1)}, bf16[16,1280]{1,0:T(8,128)(2,1)S(1)}, u32[]{:S(2)}, u32[]{:S(2)}) collective-permute-start(bf16[16,1280]{1,0:T(8,128)(2,1)S(1)} %pad_maximum_fusion.5), channel_id=1, source_target_pairs={{0,128},{8,136},{16,144},{24,152},{32,160},{40,168},{48,176},{56,1... | collective-permute-start | bytes 122888 | tf_op jit(solution)/shard_map/ppermute | solution.py:261
  155.9 9.0 %collective-permute-start.33 = (bf16[16,1280]{1,0:T(8,128)(2,1)S(1)}, bf16[16,1280]{1,0:T(8,128)(2,1)S(1)}, u32[]{:S(2)}, u32[]{:S(2)}) collective-permute-start(bf16[16,1280]{1,0:T(8,128)(2,1)S(1)} %pad_maximum_fusion.5), channel_id=1, source_target_pairs={{0,192},{8,200},{16,208},{24,216},{32,224},{40,232},{48,240},{56,2... | collective-permute-start | bytes 122888 | tf_op jit(solution)/shard_map/ppermute | solution.py:261
  155.9 9.0 %collective-permute-start.32 = (bf16[16,1280]{1,0:T(8,128)(2,1)S(1)}, bf16[16,1280]{1,0:T(8,128)(2,1)S(1)}, u32[]{:S(2)}, u32[]{:S(2)}) collective-permute-start(bf16[16,1280]{1,0:T(8,128)(2,1)S(1)} %pad_maximum_fusion.5), channel_id=1, source_target_pairs={{0,64},{8,72},{16,80},{24,88},{32,96},{40,104},{48,112},{56,120},{... | collective-permute-start | bytes 122888 | tf_op jit(solution)/shard_map/ppermute | solution.py:261
  157.9 9.0 %collective-permute-start.35 = (bf16[160,1280]{1,0:T(8,128)(2,1)S(1)}, bf16[160,1280]{1,0:T(8,128)(2,1)S(1)}, u32[]{:S(2)}, u32[]{:S(2)}) collective-permute-start(bf16[160,1280]{1,0:T(8,128)(2,1)S(1)} %pad_maximum_fusion.3.h4), channel_id=1, source_target_pairs={{0,1},{1,2},{2,3},{3,0},{4,5},{5,6},{6,7},{7,4},{8,9},{9,10},{10,1... | collective-permute-start | bytes 1228808 | tf_op jit(solution)/shard_map/ppermute | solution.py:251
  159.7 10.2 %collective-permute-start.36 = (bf16[160,1280]{1,0:T(8,128)(2,1)S(1)}, bf16[160,1280]{1,0:T(8,128)(2,1)S(1)}, u32[]{:S(2)}, u32[]{:S(2)}) collective-permute-start(bf16[160,1280]{1,0:T(8,128)(2,1)S(1)} %pad_maximum_fusion.3.h4), channel_id=1, source_target_pairs={{0,3},{1,0},{2,1},{3,2},{4,7},{5,4},{6,5},{7,6},{8,11},{9,8},{10,9... | collective-permute-start | bytes 1228808 | tf_op jit(solution)/shard_map/ppermute | solution.py:251
  164.9 19.3 %copy-start.38 = (f32[512,1280]{1,0:T(8,128)}, f32[512,1280]{1,0:T(8,128)S(1)}, u32[]{:S(2)}) copy-start(f32[512,1280]{1,0:T(8,128)S(1)} %get-tuple-element.168) | copy-start | bytes 7864324
  169.9 7.0 %collective-permute-start.39 = (bf16[64,1280]{1,0:T(8,128)(2,1)S(1)}, bf16[64,1280]{1,0:T(8,128)(2,1)S(1)}, u32[]{:S(2)}, u32[]{:S(2)}) collective-permute-start(bf16[64,1280]{1,0:T(8,128)(2,1)S(1)} %pad_maximum_fusion.4), channel_id=1, source_target_pairs={{0,32},{8,40},{16,48},{24,56},{32,0},{40,8},{48,16},{56,24},{64,96... | collective-permute-start | bytes 491528 | tf_op jit(solution)/shard_map/ppermute | solution.py:261
  170.5 8.9 %collective-permute-start.38 = (bf16[64,1280]{1,0:T(8,128)(2,1)S(1)}, bf16[64,1280]{1,0:T(8,128)(2,1)S(1)}, u32[]{:S(2)}, u32[]{:S(2)}) collective-permute-start(bf16[64,1280]{1,0:T(8,128)(2,1)S(1)} %pad_maximum_fusion.4), channel_id=1, source_target_pairs={{0,48},{8,56},{16,0},{24,8},{32,16},{40,24},{48,32},{56,40},{64,11... | collective-permute-start | bytes 491528 | tf_op jit(solution)/shard_map/ppermute | solution.py:261
  173.4 6.5 %collective-permute-start.37 = (bf16[64,1280]{1,0:T(8,128)(2,1)S(1)}, bf16[64,1280]{1,0:T(8,128)(2,1)S(1)}, u32[]{:S(2)}, u32[]{:S(2)}) collective-permute-start(bf16[64,1280]{1,0:T(8,128)(2,1)S(1)} %pad_maximum_fusion.4), channel_id=1, source_target_pairs={{0,16},{8,24},{16,32},{24,40},{32,48},{40,56},{48,0},{56,8},{64,80... | collective-permute-start | bytes 491528 | tf_op jit(solution)/shard_map/ppermute | solution.py:261
  174.3 9.2 %collective-permute-start.40 = (bf16[160,1280]{1,0:T(8,128)(2,1)S(1)}, bf16[160,1280]{1,0:T(8,128)(2,1)S(1)}, u32[]{:S(2)}, u32[]{:S(2)}) collective-permute-start(bf16[160,1280]{1,0:T(8,128)(2,1)S(1)} %collective-permute-done.36.h6), channel_id=1, source_target_pairs={{0,3},{1,0},{2,1},{3,2},{4,7},{5,4},{6,5},{7,6},{8,11},{9,8},{10,9... | collective-permute-start | bytes 1228808 | tf_op jit(solution)/shard_map/ppermute | solution.py:251
  183.4 2.5 collective-permute-start.41
  212.0 3.8 %collective-permute-start.42 = (bf16[640,640]{1,0:T(8,128)(2,1)}, bf16[640,640]{1,0:T(8,128)(2,1)}, u32[]{:S(2)}, u32[]{:S(2)}) collective-permute-start(bf16[640,640]{1,0:T(8,128)(2,1)} %get-tuple-element.138), channel_id=1, source_target_pairs={{0,8},{8,0},{16,24},{24,16},{32,40},{40,32},{48,56},{56,48},{64,72... | collective-permute-start | bytes 2457608 | tf_op jit(solution)/shard_map/ppermute | solution.py:261
  212.3 12.6 %collective-permute-start.49 = (bf16[640,640]{1,0:T(8,128)(2,1)}, bf16[640,640]{1,0:T(8,128)(2,1)S(1)}, u32[]{:S(2)}, u32[]{:S(2)}) collective-permute-start(bf16[640,640]{1,0:T(8,128)(2,1)} %copy-done.19), channel_id=1, source_target_pairs={{0,8},{8,0},{16,24},{24,16},{32,40},{40,32},{48,56},{56,48},{64,72... | collective-permute-start | bytes 2457608 | tf_op jit(solution)/shard_map/ppermute | solution.py:261
  218.2 12.0 %collective-permute-start.43 = (bf16[160,640]{1,0:T(8,128)(2,1)S(1)}, bf16[160,640]{1,0:T(8,128)(2,1)S(1)}, u32[]{:S(2)}, u32[]{:S(2)}) collective-permute-start(bf16[160,640]{1,0:T(8,128)(2,1)S(1)} %get-tuple-element.140), channel_id=1, source_target_pairs={{0,16},{8,24},{16,32},{24,40},{32,48},{40,56},{48,0},{56,8},{64,80... | collective-permute-start | bytes 614408 | tf_op jit(solution)/shard_map/ppermute | solution.py:261
  222.9 14.6 %collective-permute-start.44 = (bf16[160,640]{1,0:T(8,128)(2,1)}, bf16[160,640]{1,0:T(8,128)(2,1)}, u32[]{:S(2)}, u32[]{:S(2)}) collective-permute-start(bf16[160,640]{1,0:T(8,128)(2,1)} %get-tuple-element.141), channel_id=1, source_target_pairs={{0,48},{8,56},{16,0},{24,8},{32,16},{40,24},{48,32},{56,40},{64,11... | collective-permute-start | bytes 614408 | tf_op jit(solution)/shard_map/ppermute | solution.py:261
  224.1 13.4 %collective-permute-start.45 = (bf16[160,640]{1,0:T(8,128)(2,1)}, bf16[160,640]{1,0:T(8,128)(2,1)}, u32[]{:S(2)}, u32[]{:S(2)}) collective-permute-start(bf16[160,640]{1,0:T(8,128)(2,1)} %get-tuple-element.142), channel_id=1, source_target_pairs={{0,32},{8,40},{16,48},{24,56},{32,0},{40,8},{48,16},{56,24},{64,96... | collective-permute-start | bytes 614408 | tf_op jit(solution)/shard_map/ppermute | solution.py:261
  227.0 16.4 %collective-permute-start.50 = (bf16[160,640]{1,0:T(8,128)(2,1)}, bf16[160,640]{1,0:T(8,128)(2,1)S(1)}, u32[]{:S(2)}, u32[]{:S(2)}) collective-permute-start(bf16[160,640]{1,0:T(8,128)(2,1)} %get-tuple-element.150), channel_id=1, source_target_pairs={{0,16},{8,24},{16,32},{24,40},{32,48},{40,56},{48,0},{56,8},{64,80... | collective-permute-start | bytes 614408 | tf_op jit(solution)/shard_map/ppermute | solution.py:261
  228.1 16.8 %collective-permute-start.51 = (bf16[160,640]{1,0:T(8,128)(2,1)}, bf16[160,640]{1,0:T(8,128)(2,1)}, u32[]{:S(2)}, u32[]{:S(2)}) collective-permute-start(bf16[160,640]{1,0:T(8,128)(2,1)} %get-tuple-element.151), channel_id=1, source_target_pairs={{0,48},{8,56},{16,0},{24,8},{32,16},{40,24},{48,32},{56,40},{64,11... | collective-permute-start | bytes 614408 | tf_op jit(solution)/shard_map/ppermute | solution.py:261
  230.9 14.0 %collective-permute-start.52 = (bf16[160,640]{1,0:T(8,128)(2,1)}, bf16[160,640]{1,0:T(8,128)(2,1)}, u32[]{:S(2)}, u32[]{:S(2)}) collective-permute-start(bf16[160,640]{1,0:T(8,128)(2,1)} %get-tuple-element.152), channel_id=1, source_target_pairs={{0,32},{8,40},{16,48},{24,56},{32,0},{40,8},{48,16},{56,24},{64,96... | collective-permute-start | bytes 614408 | tf_op jit(solution)/shard_map/ppermute | solution.py:261
  240.6 10.9 %collective-permute-start.48 = (bf16[40,640]{1,0:T(8,128)(2,1)S(1)}, bf16[40,640]{1,0:T(8,128)(2,1)S(1)}, u32[]{:S(2)}, u32[]{:S(2)}) collective-permute-start(bf16[40,640]{1,0:T(8,128)(2,1)S(1)} %get-tuple-element.146), channel_id=1, source_target_pairs={{0,128},{8,136},{16,144},{24,152},{32,160},{40,168},{48,176},{56,1... | collective-permute-start | bytes 153608 | tf_op jit(solution)/shard_map/ppermute | solution.py:261
  241.0 10.6 %collective-permute-start.47 = (bf16[40,640]{1,0:T(8,128)(2,1)S(1)}, bf16[40,640]{1,0:T(8,128)(2,1)S(1)}, u32[]{:S(2)}, u32[]{:S(2)}) collective-permute-start(bf16[40,640]{1,0:T(8,128)(2,1)S(1)} %get-tuple-element.145), channel_id=1, source_target_pairs={{0,192},{8,200},{16,208},{24,216},{32,224},{40,232},{48,240},{56,2... | collective-permute-start | bytes 153608 | tf_op jit(solution)/shard_map/ppermute | solution.py:261
  243.4 8.2 %collective-permute-start.46 = (bf16[40,640]{1,0:T(8,128)(2,1)S(1)}, bf16[40,640]{1,0:T(8,128)(2,1)S(1)}, u32[]{:S(2)}, u32[]{:S(2)}) collective-permute-start(bf16[40,640]{1,0:T(8,128)(2,1)S(1)} %get-tuple-element.144), channel_id=1, source_target_pairs={{0,64},{8,72},{16,80},{24,88},{32,96},{40,104},{48,112},{56,120},{... | collective-permute-start | bytes 153608 | tf_op jit(solution)/shard_map/ppermute | solution.py:261
  247.1 5.2 %collective-permute-start.55 = (bf16[40,640]{1,0:T(8,128)(2,1)S(1)}, bf16[40,640]{1,0:T(8,128)(2,1)S(1)}, u32[]{:S(2)}, u32[]{:S(2)}) collective-permute-start(bf16[40,640]{1,0:T(8,128)(2,1)S(1)} %get-tuple-element.156), channel_id=1, source_target_pairs={{0,128},{8,136},{16,144},{24,152},{32,160},{40,168},{48,176},{56,1... | collective-permute-start | bytes 153608 | tf_op jit(solution)/shard_map/ppermute | solution.py:261
  249.5 4.5 %collective-permute-start.54 = (bf16[40,640]{1,0:T(8,128)(2,1)S(1)}, bf16[40,640]{1,0:T(8,128)(2,1)S(1)}, u32[]{:S(2)}, u32[]{:S(2)}) collective-permute-start(bf16[40,640]{1,0:T(8,128)(2,1)S(1)} %get-tuple-element.155), channel_id=1, source_target_pairs={{0,192},{8,200},{16,208},{24,216},{32,224},{40,232},{48,240},{56,2... | collective-permute-start | bytes 153608 | tf_op jit(solution)/shard_map/ppermute | solution.py:261
  251.5 5.9 %collective-permute-start.53 = (bf16[40,640]{1,0:T(8,128)(2,1)S(1)}, bf16[40,640]{1,0:T(8,128)(2,1)S(1)}, u32[]{:S(2)}, u32[]{:S(2)}) collective-permute-start(bf16[40,640]{1,0:T(8,128)(2,1)S(1)} %get-tuple-element.154), channel_id=1, source_target_pairs={{0,64},{8,72},{16,80},{24,88},{32,96},{40,104},{48,112},{56,120},{... | collective-permute-start | bytes 153608 | tf_op jit(solution)/shard_map/ppermute | solution.py:261
  (39 other events, 160.4 us)
where the time goes:
time: 262 us; the launch traced here: 258 us
  starting transfers between devices  102 us (39%)
  waiting for transfers between devices  75.3 us (29%)
  Pallas kernels  30.9 us (12%)
  matrix products  20.5 us (8%)
  local copies, waits for them, and re-layouts  19.3 us (7%)
  other arithmetic  6.98 us (3%)
  between operations  3.38 us (1%)
    ppermute x28, waiting for transfers between devices, move_txt(): return lax.ppermute(value, 'txt', pairs)  61.2 us
    ppermute x28, starting transfers between devices, move_txt(): return lax.ppermute(value, 'txt', pairs)  58.7 us
    ppermute x28, starting transfers between devices, move_img(): return lax.ppermute(value, 'img', pairs)  43.2 us
    pallas_call x13, Pallas kernels, call(): pl.pallas_call(kernel, out_shape=outs, in_specs=specs, out_specs=[pl.Bloc...  30.9 us
    unnamed x96, local copies, waits for them, and re-layouts  16.6 us
    ppermute x28, waiting for transfers between devices, move_img(): return lax.ppermute(value, 'img', pairs)  14.1 us
  transfers between devices with their start and end apart: 56, of which 23 were waited for; matrix products, arithmetic and copies ran while one was open for 8% of the time, Pallas kernels for 4%

commit v1 on v0

--- a/solution.py
+++ b/solution.py
@@ -443,9 +443,11 @@
     lengths = image_all[: 8 * samples, image_width + 1].astype(jnp.int32)
     image_centred = centre(image_all[:, :image_width].astype(F32))
     image_normed = (image_centred * inv_std_of(image_centred) * image_gain).astype(BF)
+    (image_normed,) = together(image_normed)
     image_raw = jnp.dot(image_normed, image_proj, preferred_element_type=F32)
     image_unit, image_inv = unit_rows(image_raw)
     image_send = image_unit.astype(BF)
+    image_low = (image_unit - lax.reduce_precision(image_unit, 8, 7)).astype(BF)
 
     pooled_all = gather_core(pooled_y)
 
@@ -521,19 +523,30 @@
     down_grad = sum_img_end(down_terms, z_at).T
     up_grad = sum_img_end(up_terms, z_at)
 
-    grad_image_unit = logit_scale * (
-        lax.dot_general(grad_high, text_send, OVER_ROWS, preferred_element_type=F32)
-        + lax.dot_general(grad_low, text_send, OVER_ROWS, preferred_element_type=F32)
-    )
-    grad_image_raw = unit_back(grad_image_unit, image_unit, image_inv).astype(BF)
-    columns = grad_image_raw.shape[1] // 32
-    chosen = jnp.arange(grad_image_raw.shape[1])[:, None] == (
+    columns = image_unit.shape[1] // 32
+    chosen = jnp.arange(image_unit.shape[1])[:, None] == (
         img * columns + jnp.arange(columns)[None, :]
     )
-    own_columns = jnp.dot(
-        grad_image_raw, chosen.astype(BF), preferred_element_type=F32
+    chosen = chosen.astype(BF)
+    pick_columns = (((0,), (1,)), ((), ()))
+    text_columns = lax.dot_general(
+        chosen, text_send, pick_columns, preferred_element_type=F32
     ).astype(BF)
-    projected = lax.dot_general(image_normed, own_columns, OVER_ROWS, preferred_element_type=F32)
+    unit_columns = lax.dot_general(
+        chosen, image_send, pick_columns, preferred_element_type=F32
+    ) + lax.dot_general(chosen, image_low, pick_columns, preferred_element_type=F32)
+    rest = logit_scale * lax.dot_general(
+        text_send, image_low, OVER_COLS, preferred_element_type=F32
+    )
+    along = jnp.sum(grad_scores * (scores + rest), axis=0, keepdims=True)
+    grad_columns = logit_scale * (
+        jnp.dot(text_columns, grad_high, preferred_element_type=F32)
+        + jnp.dot(text_columns, grad_low, preferred_element_type=F32)
+    )
+    own_columns = (image_inv.reshape(1, batch) * (grad_columns - unit_columns * along)).astype(BF)
+    projected = lax.dot_general(
+        image_normed, own_columns, (((0,), (1,)), ((), ())), preferred_element_type=F32
+    )
     rows = image_width // 8
     image_proj_grad = lax.dynamic_slice_in_dim(projected, txt * rows, rows, axis=0)
     return (image_proj_grad, up_grad, down_grad)

time: 262 us -> 253 us (0.966)
  the two profiles are of different devices: /device:TPU:6 before, /device:TPU:8 now
where the time goes in v1:
time: 253 us; the launch traced here: 249 us
  starting transfers between devices  104 us (41%)
  waiting for transfers between devices  70.6 us (28%)
  Pallas kernels  28.7 us (11%)
  matrix products  17.5 us (7%)
  local copies, waits for them, and re-layouts  16.3 us (6%)
  other arithmetic  7.61 us (3%)
  between operations  3.56 us (1%)
    ppermute x28, starting transfers between devices, move_txt(): return lax.ppermute(value, 'txt', pairs)  61.7 us
    ppermute x28, waiting for transfers between devices, move_txt(): return lax.ppermute(value, 'txt', pairs)  60.7 us
    ppermute x28, starting transfers between devices, move_img(): return lax.ppermute(value, 'img', pairs)  42.7 us
    pallas_call x13, Pallas kernels, call(): pl.pallas_call(kernel, out_shape=outs, in_specs=specs, out_specs=[pl.Bloc...  28.7 us
    unnamed x76, local copies, waits for them, and re-layouts  13.4 us
    ppermute x28, waiting for transfers between devices, move_img(): return lax.ppermute(value, 'img', pairs)  9.84 us
  transfers between devices with their start and end apart: 56, of which 23 were waited for; matrix products, arithmetic and copies ran while one was open for 8% of the time, Pallas kernels for 3%

profile of v1, /device:TPU:8, one launch (start us, length us, event | category | flops | bytes accessed | tf_op | source)
XLA Modules:
  0.0 248.5 jit_solution(15210979926705582625)
XLA Ops:
  5.7 2.8 %collective-permute-start.1 = (bf16[160,1280]{1,0:T(8,128)(2,1)S(1)}, bf16[160,1280]{1,0:T(8,128)(2,1)S(1)}, u32[]{:S(2)}, u32[]{:S(2)}) collective-permute-start(bf16[160,1280]{1,0:T(8,128)(2,1)S(1)} %shard_map.139.own_ref), channel_id=1, source_target_pairs={{0,3},{1,0},{2,1},{3,2},{4,7},{5,4},{6,5},{7,6},{8,11},{9,8},{10,9... | collective-permute-start | bytes 1228808 | tf_op jit(solution)/shard_map/ppermute | solution.py:251
  8.5 7.2 %collective-permute-start.7 = (bf16[160,1280]{1,0:T(8,128)(2,1)S(1)}, bf16[160,1280]{1,0:T(8,128)(2,1)S(1)}, u32[]{:S(2)}, u32[]{:S(2)}) collective-permute-start(bf16[160,1280]{1,0:T(8,128)(2,1)S(1)} %shard_map.139.own_ref), channel_id=1, source_target_pairs={{0,4},{1,5},{2,6},{3,7},{4,0},{5,1},{6,2},{7,3},{8,12},{9,13},{10,... | collective-permute-start | bytes 1228808 | tf_op jit(solution)/shard_map/ppermute | solution.py:251
  15.7 1.5 collective-permute-done.1.right_ref
  18.4 13.9 %collective-permute-done.7 = bf16[160,1280]{1,0:T(8,128)(2,1)S(1)} collective-permute-done((bf16[160,1280]{1,0:T(8,128)(2,1)S(1)}, bf16[160,1280]{1,0:T(8,128)(2,1)S(1)}, u32[]{:S(2)}, u32[]{:S(2)}) %collective-permute-start.7) | collective-permute-done | bytes 409632 | tf_op jit(solution)/shard_map/ppermute | solution.py:251
  33.2 1.2 collective-permute-start.2
  34.5 8.7 %collective-permute-done.9.right_ref = bf16[160,1280]{1,0:T(8,128)(2,1)S(1)} collective-permute-done((bf16[160,1280]{1,0:T(8,128)(2,1)S(1)}, bf16[160,1280]{1,0:T(8,128)(2,1)S(1)}, u32[]{:S(2)}, u32[]{:S(2)}) %collective-permute-start.9) | collective-permute-done | bytes 409632 | tf_op jit(solution)/shard_map/ppermute | solution.py:251
  43.2 3.2 %collective-permute-start.10 = (bf16[160,1280]{1,0:T(8,128)(2,1)S(1)}, bf16[160,1280]{1,0:T(8,128)(2,1)S(1)}, u32[]{:S(2)}, u32[]{:S(2)}) collective-permute-start(bf16[160,1280]{1,0:T(8,128)(2,1)S(1)} %collective-permute-done.9.right_ref), channel_id=1, source_target_pairs={{0,3},{1,0},{2,1},{3,2},{4,7},{5,4},{6,5},{7,6},{8,11},{9,8},{10,9... | collective-permute-start | bytes 1228808 | tf_op jit(solution)/shard_map/ppermute | solution.py:251
  46.4 1.4 copy-done.10
  47.9 1.4 copy-done.12
  49.3 3.4 %shard_map.140 = (bf16[640,1280]{1,0:T(8,128)(2,1)S(1)}, bf16[640,640]{1,0:T(8,128)(2,1)S(1)}, bf16[640,640]{1,0:T(8,128)(2,1)S(1)}, bf16[8,1792]{1,0:T(8,128)(2...) custom-call(bf16[160,1280]{1,0:T(8,128)(2,1)S(1)} %shard_map.139.own, ...), custom_call_target="tpu_custom_call" | custom-call | flops 2097152000 | bytes 11087872 | tf_op jit(solution)/shard_map/pallas_call | solution.py:47
  53.9 3.4 %shard_map.142 = (bf16[640,1280]{1,0:T(8,128)(2,1)S(1)}, bf16[640,640]{1,0:T(8,128)(2,1)S(1)}, bf16[640,640]{1,0:T(8,128)(2,1)S(1)}, bf16[8,1792]{1,0:T(8,128)(2...) custom-call(bf16[160,1280]{1,0:T(8,128)(2,1)S(1)} %broadcast_add_fus, ...), custom_call_target="tpu_custom_call" | custom-call | flops 2097152000 | bytes 11087872 | tf_op jit(solution)/shard_map/pallas_call | solution.py:47
  57.4 3.0 %collective-permute-start.13 = (bf16[16,1792]{1,0:T(8,128)(2,1)S(1)}, bf16[16,1792]{1,0:T(8,128)(2,1)S(1)}, u32[]{:S(2)}, u32[]{:S(2)}) collective-permute-start(bf16[16,1792]{1,0:T(8,128)(2,1)S(1)} %get-tuple-element.163), channel_id=1, source_target_pairs={{0,64},{8,72},{16,80},{24,88},{32,96},{40,104},{48,112},{56,120},{... | collective-permute-start | bytes 172040 | tf_op jit(solution)/shard_map/ppermute | solution.py:261
  61.4 2.8 %collective-permute-start.14 = (bf16[16,1792]{1,0:T(8,128)(2,1)S(1)}, bf16[16,1792]{1,0:T(8,128)(2,1)S(1)}, u32[]{:S(2)}, u32[]{:S(2)}) collective-permute-start(bf16[16,1792]{1,0:T(8,128)(2,1)S(1)} %get-tuple-element.163), channel_id=1, source_target_pairs={{0,192},{8,200},{16,208},{24,216},{32,224},{40,232},{48,240},{56,2... | collective-permute-start | bytes 172040 | tf_op jit(solution)/shard_map/ppermute | solution.py:261
  64.2 3.2 %collective-permute-start.12 = (bf16[80,1280]{1,0:T(8,128)(2,1)S(1)}, bf16[80,1280]{1,0:T(8,128)(2,1)S(1)}, u32[]{:S(2)}, u32[]{:S(2)}) collective-permute-start(bf16[80,1280]{1,0:T(8,128)(2,1)S(1)} %get-tuple-element.91), channel_id=1, source_target_pairs={{0,3},{1,0},{2,1},{3,2},{4,7},{5,4},{6,5},{7,6},{8,11},{9,8},{10,9... | collective-permute-start | bytes 614408 | tf_op jit(solution)/shard_map/ppermute | solution.py:251
  67.5 4.2 %collective-permute-done.11.got_a_ref = bf16[80,1280]{1,0:T(8,128)(2,1)S(1)} collective-permute-done((bf16[80,1280]{1,0:T(8,128)(2,1)S(1)}, bf16[80,1280]{1,0:T(8,128)(2,1)S(1)}, u32[]{:S(2)}, u32[]{:S(2)}) %collective-permute-start.11) | collective-permute-done | bytes 204832 | tf_op jit(solution)/shard_map/ppermute | solution.py:251
  72.0 3.5 %collective-permute-start.17 = (bf16[160,1280]{1,0:T(8,128)(2,1)S(1)}, bf16[160,1280]{1,0:T(8,128)(2,1)S(1)}, u32[]{:S(2)}, u32[]{:S(2)}) collective-permute-start(bf16[160,1280]{1,0:T(8,128)(2,1)S(1)} %get-tuple-element.97), channel_id=1, source_target_pairs={{0,3},{1,0},{2,1},{3,2},{4,7},{5,4},{6,5},{7,6},{8,11},{9,8},{10,9... | collective-permute-start | bytes 1228808 | tf_op jit(solution)/shard_map/ppermute | solution.py:251
  75.5 3.2 %collective-permute-start.4 = (bf16[80,1280]{1,0:T(8,128)(2,1)S(1)}, bf16[80,1280]{1,0:T(8,128)(2,1)S(1)}, u32[]{:S(2)}, u32[]{:S(2)}) collective-permute-start(bf16[80,1280]{1,0:T(8,128)(2,1)S(1)} %get-tuple-element.84), channel_id=1, source_target_pairs={{0,3},{1,0},{2,1},{3,2},{4,7},{5,4},{6,5},{7,6},{8,11},{9,8},{10,9... | collective-permute-start | bytes 614408 | tf_op jit(solution)/shard_map/ppermute | solution.py:251
  78.7 2.3 collective-permute-start.21
  81.0 3.3 %collective-permute-done.3.got_a_ref = bf16[80,1280]{1,0:T(8,128)(2,1)S(1)} collective-permute-done((bf16[80,1280]{1,0:T(8,128)(2,1)S(1)}, bf16[80,1280]{1,0:T(8,128)(2,1)S(1)}, u32[]{:S(2)}, u32[]{:S(2)}) %collective-permute-start.3) | collective-permute-done | bytes 204832 | tf_op jit(solution)/shard_map/ppermute | solution.py:251
  84.8 1.6 collective-permute-start.19
  86.7 5.3 %collective-permute-start.18 = (bf16[160,1280]{1,0:T(8,128)(2,1)S(1)}, bf16[160,1280]{1,0:T(8,128)(2,1)S(1)}, u32[]{:S(2)}, u32[]{:S(2)}) collective-permute-start(bf16[160,1280]{1,0:T(8,128)(2,1)S(1)} %shard_map.144), channel_id=1, source_target_pairs={{0,4},{1,5},{2,6},{3,7},{4,0},{5,1},{6,2},{7,3},{8,12},{9,13},{10,... | collective-permute-start | bytes 1228808 | tf_op jit(solution)/shard_map/ppermute | solution.py:251
  92.5 2.7 %collective-permute-start.6 = (bf16[160,1280]{1,0:T(8,128)(2,1)S(1)}, bf16[160,1280]{1,0:T(8,128)(2,1)S(1)}, u32[]{:S(2)}, u32[]{:S(2)}) collective-permute-start(bf16[160,1280]{1,0:T(8,128)(2,1)S(1)} %get-tuple-element.86), channel_id=1, source_target_pairs={{0,3},{1,0},{2,1},{3,2},{4,7},{5,4},{6,5},{7,6},{8,11},{9,8},{10,9... | collective-permute-start | bytes 1228808 | tf_op jit(solution)/shard_map/ppermute | solution.py:251
  96.3 5.2 %collective-permute-done.18.away_ref = bf16[160,1280]{1,0:T(8,128)(2,1)S(1)} collective-permute-done((bf16[160,1280]{1,0:T(8,128)(2,1)S(1)}, bf16[160,1280]{1,0:T(8,128)(2,1)S(1)}, u32[]{:S(2)}, u32[]{:S(2)}) %collective-permute-start.18) | collective-permute-done | bytes 409632 | tf_op jit(solution)/shard_map/ppermute | solution.py:251
  104.0 2.7 %collective-permute-start.24 = (bf16[2,1280]{1,0:T(2,128)(2,1)S(1)}, bf16[2,1280]{1,0:T(2,128)(2,1)S(1)}, u32[]{:S(2)}, u32[]{:S(2)}) collective-permute-start(bf16[2,1280]{1,0:T(2,128)(2,1)S(1)} %get-tuple-element.105), channel_id=1, source_target_pairs={{0,2},{1,3},{2,0},{3,1},{4,6},{5,7},{6,4},{7,5},{8,10},{9,11},{10,... | collective-permute-start | bytes 15368 | tf_op jit(solution)/shard_map/ppermute | solution.py:251
  106.7 9.6 %collective-permute-start.23 = (bf16[2,1280]{1,0:T(2,128)(2,1)S(1)}, bf16[2,1280]{1,0:T(2,128)(2,1)S(1)}, u32[]{:S(2)}, u32[]{:S(2)}) collective-permute-start(bf16[2,1280]{1,0:T(2,128)(2,1)S(1)} %get-tuple-element.105), channel_id=1, source_target_pairs={{0,3},{1,0},{2,1},{3,2},{4,7},{5,4},{6,5},{7,6},{8,11},{9,8},{10,9... | collective-permute-start | bytes 15368 | tf_op jit(solution)/shard_map/ppermute | solution.py:251
  118.0 2.3 collective-permute-start.26
  120.3 3.7 %collective-permute-start.27 = (bf16[80,1280]{1,0:T(8,128)(2,1)}, bf16[80,1280]{1,0:T(8,128)(2,1)S(1)}, u32[]{:S(2)}, u32[]{:S(2)}) collective-permute-start(bf16[80,1280]{1,0:T(8,128)(2,1)} %copy-done.17), channel_id=1, source_target_pairs={{0,4},{1,5},{2,6},{3,7},{4,0},{5,1},{6,2},{7,3},{8,12},{9,13},{10,... | collective-permute-start | bytes 614408 | tf_op jit(solution)/shard_map/ppermute | solution.py:251
  124.0 1.6 pad_maximum_fusion
  125.6 5.3 %collective-permute-done.27 = bf16[80,1280]{1,0:T(8,128)(2,1)S(1)} collective-permute-done((bf16[80,1280]{1,0:T(8,128)(2,1)}, bf16[80,1280]{1,0:T(8,128)(2,1)S(1)}, u32[]{:S(2)}, u32[]{:S(2)}) %collective-permute-start.27) | collective-permute-done | bytes 204832 | tf_op jit(solution)/shard_map/ppermute | solution.py:251
  131.0 1.5 collective-permute-done.25.h1
  134.0 4.0 %collective-permute-start.29 = (bf16[8,1280]{1,0:T(8,128)(2,1)S(1)}, bf16[8,1280]{1,0:T(8,128)(2,1)S(1)}, u32[]{:S(2)}, u32[]{:S(2)}) collective-permute-start(bf16[8,1280]{1,0:T(8,128)(2,1)S(1)} %pad_maximum_fusion.6), channel_id=1, source_target_pairs={{0,4},{1,5},{2,6},{3,7},{4,0},{5,1},{6,2},{7,3},{8,12},{9,13},{10,... | collective-permute-start | bytes 61448 | tf_op jit(solution)/shard_map/ppermute | solution.py:251
  137.9 2.1 collective-permute-start.31
  140.0 4.9 %multiply_reduce_fusion.1 = (f32[512]{0:T(512)S(1)}, f32[512,1280]{1,0:T(8,128)S(1)}) fusion(bf16[512,1664]{1,0:T(8,128)(2,1)S(1)} %fusion.4, bf16[1664,1280]{1,0:T(8,128)(2,1)} %param.22), kind=kOutput, calls=%fused_computation.10 | convolution fusion | flops 2182348288 | bytes 8587264 | tf_op jit(solution)/shard_map/dot_general | solution.py:447
  144.9 2.9 %collective-permute-done.31 = bf16[80,1280]{1,0:T(8,128)(2,1)S(1)} collective-permute-done((bf16[80,1280]{1,0:T(8,128)(2,1)S(1)}, bf16[80,1280]{1,0:T(8,128)(2,1)S(1)}, u32[]{:S(2)}, u32[]{:S(2)}) %collective-permute-start.31) | collective-permute-done | bytes 204832 | tf_op jit(solution)/shard_map/ppermute | solution.py:251
  147.9 2.6 %collective-permute-done.30.h3 = bf16[160,1280]{1,0:T(8,128)(2,1)S(1)} collective-permute-done((bf16[160,1280]{1,0:T(8,128)(2,1)S(1)}, bf16[160,1280]{1,0:T(8,128)(2,1)S(1)}, u32[]{:S(2)}, u32[]{:S(2)}) %collective-permute-start.30) | collective-permute-done | bytes 409632 | tf_op jit(solution)/shard_map/ppermute | solution.py:251
  150.5 6.7 %collective-permute-start.34 = (bf16[16,1280]{1,0:T(8,128)(2,1)S(1)}, bf16[16,1280]{1,0:T(8,128)(2,1)S(1)}, u32[]{:S(2)}, u32[]{:S(2)}) collective-permute-start(bf16[16,1280]{1,0:T(8,128)(2,1)S(1)} %pad_maximum_fusion.5), channel_id=1, source_target_pairs={{0,128},{8,136},{16,144},{24,152},{32,160},{40,168},{48,176},{56,1... | collective-permute-start | bytes 122888 | tf_op jit(solution)/shard_map/ppermute | solution.py:261
  157.8 1.4 collective-permute-start.32
  159.2 1.7 collective-permute-start.36
  161.5 2.2 collective-permute-done.32
  163.7 4.6 %collective-permute-done.36.h6 = bf16[160,1280]{1,0:T(8,128)(2,1)S(1)} collective-permute-done((bf16[160,1280]{1,0:T(8,128)(2,1)S(1)}, bf16[160,1280]{1,0:T(8,128)(2,1)S(1)}, u32[]{:S(2)}, u32[]{:S(2)}) %collective-permute-start.36) | collective-permute-done | bytes 409632 | tf_op jit(solution)/shard_map/ppermute | solution.py:251
  168.3 2.6 %collective-permute-done.35.h5 = bf16[160,1280]{1,0:T(8,128)(2,1)S(1)} collective-permute-done((bf16[160,1280]{1,0:T(8,128)(2,1)S(1)}, bf16[160,1280]{1,0:T(8,128)(2,1)S(1)}, u32[]{:S(2)}, u32[]{:S(2)}) %collective-permute-start.35) | collective-permute-done | bytes 409632 | tf_op jit(solution)/shard_map/ppermute | solution.py:251
  170.9 3.4 %collective-permute-start.39 = (bf16[64,1280]{1,0:T(8,128)(2,1)S(1)}, bf16[64,1280]{1,0:T(8,128)(2,1)S(1)}, u32[]{:S(2)}, u32[]{:S(2)}) collective-permute-start(bf16[64,1280]{1,0:T(8,128)(2,1)S(1)} %pad_maximum_fusion.4), channel_id=1, source_target_pairs={{0,32},{8,40},{16,48},{24,56},{32,0},{40,8},{48,16},{56,24},{64,96... | collective-permute-start | bytes 491528 | tf_op jit(solution)/shard_map/ppermute | solution.py:261
  174.6 1.6 collective-permute-start.37
  176.9 1.2 collective-permute-done.39
  178.1 1.7 collective-permute-done.38
  180.0 4.2 %collective-permute-done.40.h7 = bf16[160,1280]{1,0:T(8,128)(2,1)S(1)} collective-permute-done((bf16[160,1280]{1,0:T(8,128)(2,1)S(1)}, bf16[160,1280]{1,0:T(8,128)(2,1)S(1)}, u32[]{:S(2)}, u32[]{:S(2)}) %collective-permute-start.40) | collective-permute-done | bytes 409632 | tf_op jit(solution)/shard_map/ppermute | solution.py:251
  186.3 2.0 multiply_reduce_fusion
  193.4 9.2 %shard_map.146 = (bf16[1280,1280]{1,0:T(8,128)(2,1)S(1)}, bf16[640,640]{1,0:T(8,128)(2,1)S(1)}, bf16[640,640]{1,0:T(8,128)(2,1)S(1)}) custom-call(s32[1]{0:T(128)} %bitcast.3.core_ref, s32[16]{0:T(128)S(1)} %convert_reduce_fusion.1.length_ref, bf16[160,1280]{1,0:T(8,128)(2,1)S(1)} %copy-done.16, bf16[160,1280]{1,0:T(8,128)(2,1)S(1)} %collective-permute-done.25.h1, ...), custom_call_target="tpu_custom_call" | custom-call | flops 2097152000 | bytes 9912388 | tf_op jit(solution)/shard_map/pallas_call | solution.py:47
  202.7 5.7 %shard_map.147 = (bf16[640,640]{1,0:T(8,128)(2,1)S(1)}, bf16[640,640]{1,0:T(8,128)(2,1)S(1)}) custom-call(s32[1]{0:T(128)} %bitcast.3.core_ref, bf16[1280,1280]{1,0:T(8,128)(2,1)S(1)} %get-tuple-element.132.grad_ref, bf16[640,1280]{1,0:T(8,128)(2,1)S(1)} %copy-done.14, bf16[640,640]{1,0:T(8,128)(2,1)S(1)} %copy-done.27, bf16[640,640]{1,0:T(8,128)(2,1)S(1)} %copy-done.29, ...), custom_call_target="tpu_custom_call" | custom-call | flops 4194304000 | bytes 11468804 | tf_op jit(solution)/shard_map/pallas_call | solution.py:47
  210.1 1.4 fusion.13
  211.5 1.2 shard_map.148
  213.6 2.0 collective-permute-start.44
  215.6 1.8 collective-permute-start.45
  219.3 1.3 collective-permute-start.50
  222.0 1.8 collective-permute-start.52
  223.8 3.8 %fusion.19 = f32[1664,40]{0,1:T(8,128)} fusion(bf16[512,1664]{1,0:T(8,128)(2,1)} %copy-done.32, f32[40,512]{1,0:T(8,128)} %fusion.17, f32[40,512]{1,0:T(8,128)} %fusion.29, s32[40]{0:T(128)S(1)} %iota_add_fusion, f32[512]{0:T(512)S(1)} %fusion.13, f32[512]{0:T(512)S(1)} %add_rsqrt_fusion.1, f32[512,1280]{1,0:T(8,128)} %copy-done.30), kind=kOutput, calls=%fused_computation.39 | convolution fusion | flops 123412480 | bytes 4759712 | tf_op jit(solution)/shard_map/dot_general | solution.py:547
  230.0 1.2 shard_map.149
  231.1 1.2 collective-permute-start.46
  232.3 2.7 %collective-permute-start.47 = (bf16[40,640]{1,0:T(8,128)(2,1)S(1)}, bf16[40,640]{1,0:T(8,128)(2,1)S(1)}, u32[]{:S(2)}, u32[]{:S(2)}) collective-permute-start(bf16[40,640]{1,0:T(8,128)(2,1)S(1)} %get-tuple-element.145), channel_id=1, source_target_pairs={{0,192},{8,200},{16,208},{24,216},{32,224},{40,232},{48,240},{56,2... | collective-permute-start | bytes 153608 | tf_op jit(solution)/shard_map/ppermute | solution.py:261
  235.1 1.5 constant_dynamic-slice_fusion
  237.6 1.2 shard_map.151
  238.8 1.5 collective-permute-start.53
  240.2 2.4 collective-permute-start.54
  245.3 2.3 collective-permute-done.55
  (182 shorter events, 37.8 us)
Async XLA Ops:
  0.6 185.7 %copy-start = (bf16[1280,1280]{1,0:T(8,128)(2,1)S(1)}, bf16[1280,1280]{1,0:T(8,128)(2,1)}, u32[]{:S(2)}) copy-start(bf16[1280,1280]{1,0:T(8,128)(2,1)} %param.19) | copy-start | bytes 9830404
  5.7 11.6 %collective-permute-start.1 = (bf16[160,1280]{1,0:T(8,128)(2,1)S(1)}, bf16[160,1280]{1,0:T(8,128)(2,1)S(1)}, u32[]{:S(2)}, u32[]{:S(2)}) collective-permute-start(bf16[160,1280]{1,0:T(8,128)(2,1)S(1)} %shard_map.139.own_ref), channel_id=1, source_target_pairs={{0,3},{1,0},{2,1},{3,2},{4,7},{5,4},{6,5},{7,6},{8,11},{9,8},{10,9... | collective-permute-start | bytes 1228808 | tf_op jit(solution)/shard_map/ppermute | solution.py:251
  8.5 23.8 %collective-permute-start.7 = (bf16[160,1280]{1,0:T(8,128)(2,1)S(1)}, bf16[160,1280]{1,0:T(8,128)(2,1)S(1)}, u32[]{:S(2)}, u32[]{:S(2)}) collective-permute-start(bf16[160,1280]{1,0:T(8,128)(2,1)S(1)} %shard_map.139.own_ref), channel_id=1, source_target_pairs={{0,4},{1,5},{2,6},{3,7},{4,0},{5,1},{6,2},{7,3},{8,12},{9,13},{10,... | collective-permute-start | bytes 1228808 | tf_op jit(solution)/shard_map/ppermute | solution.py:251
  15.7 17.5 %collective-permute-start = (bf16[160,1280]{1,0:T(8,128)(2,1)S(1)}, bf16[160,1280]{1,0:T(8,128)(2,1)S(1)}, u32[]{:S(2)}, u32[]{:S(2)}) collective-permute-start(bf16[160,1280]{1,0:T(8,128)(2,1)S(1)} %shard_map.139.own_ref), channel_id=1, source_target_pairs={{0,1},{1,2},{2,3},{3,0},{4,5},{5,6},{6,7},{7,4},{8,9},{9,10},{10,1... | collective-permute-start | bytes 1228808 | tf_op jit(solution)/shard_map/ppermute | solution.py:251
  32.3 10.9 %collective-permute-start.9 = (bf16[160,1280]{1,0:T(8,128)(2,1)S(1)}, bf16[160,1280]{1,0:T(8,128)(2,1)S(1)}, u32[]{:S(2)}, u32[]{:S(2)}) collective-permute-start(bf16[160,1280]{1,0:T(8,128)(2,1)S(1)} %broadcast_add_fusion.own_ref), channel_id=1, source_target_pairs={{0,3},{1,0},{2,1},{3,2},{4,7},{5,4},{6,5},{7,6},{8,11},{9,8},{10,9... | collective-permute-start | bytes 1228808 | tf_op jit(solution)/shard_map/ppermute | solution.py:251
  33.2 13.2 %collective-permute-start.2 = (bf16[160,1280]{1,0:T(8,128)(2,1)S(1)}, bf16[160,1280]{1,0:T(8,128)(2,1)S(1)}, u32[]{:S(2)}, u32[]{:S(2)}) collective-permute-start(bf16[160,1280]{1,0:T(8,128)(2,1)S(1)} %collective-permute-done.left_ref), channel_id=1, source_target_pairs={{0,1},{1,2},{2,3},{3,0},{4,5},{5,6},{6,7},{7,4},{8,9},{9,10},{10,1... | collective-permute-start | bytes 1228808 | tf_op jit(solution)/shard_map/ppermute | solution.py:251
  34.4 19.5 %collective-permute-start.8 = (bf16[160,1280]{1,0:T(8,128)(2,1)S(1)}, bf16[160,1280]{1,0:T(8,128)(2,1)S(1)}, u32[]{:S(2)}, u32[]{:S(2)}) collective-permute-start(bf16[160,1280]{1,0:T(8,128)(2,1)S(1)} %broadcast_add_fusion.own_ref), channel_id=1, source_target_pairs={{0,1},{1,2},{2,3},{3,0},{4,5},{5,6},{6,7},{7,4},{8,9},{9,10},{10,1... | collective-permute-start | bytes 1228808 | tf_op jit(solution)/shard_map/ppermute | solution.py:251
  43.2 10.7 %collective-permute-start.10 = (bf16[160,1280]{1,0:T(8,128)(2,1)S(1)}, bf16[160,1280]{1,0:T(8,128)(2,1)S(1)}, u32[]{:S(2)}, u32[]{:S(2)}) collective-permute-start(bf16[160,1280]{1,0:T(8,128)(2,1)S(1)} %collective-permute-done.9.right_ref), channel_id=1, source_target_pairs={{0,3},{1,0},{2,1},{3,2},{4,7},{5,4},{6,5},{7,6},{8,11},{9,8},{10,9... | collective-permute-start | bytes 1228808 | tf_op jit(solution)/shard_map/ppermute | solution.py:251
  57.3 29.2 %copy-start.20 = (bf16[640,1280]{1,0:T(8,128)(2,1)}, bf16[640,1280]{1,0:T(8,128)(2,1)S(1)}, u32[]{:S(2)}) copy-start(bf16[640,1280]{1,0:T(8,128)(2,1)S(1)} %get-tuple-element.136.normed_b_ref) | copy-start | bytes 4915204
  57.3 29.2 %copy-start.24 = (bf16[640,640]{1,0:T(8,128)(2,1)}, bf16[640,640]{1,0:T(8,128)(2,1)S(1)}, u32[]{:S(2)}) copy-start(bf16[640,640]{1,0:T(8,128)(2,1)S(1)} %get-tuple-element.131.act_b_ref) | copy-start | bytes 2457604
  57.3 29.2 %copy-start.28 = (bf16[640,640]{1,0:T(8,128)(2,1)}, bf16[640,640]{1,0:T(8,128)(2,1)S(1)}, u32[]{:S(2)}) copy-start(bf16[640,640]{1,0:T(8,128)(2,1)S(1)} %get-tuple-element.134.slope_b_ref) | copy-start | bytes 2457604
  57.4 10.1 %collective-permute-start.13 = (bf16[16,1792]{1,0:T(8,128)(2,1)S(1)}, bf16[16,1792]{1,0:T(8,128)(2,1)S(1)}, u32[]{:S(2)}, u32[]{:S(2)}) collective-permute-start(bf16[16,1792]{1,0:T(8,128)(2,1)S(1)} %get-tuple-element.163), channel_id=1, source_target_pairs={{0,64},{8,72},{16,80},{24,88},{32,96},{40,104},{48,112},{56,120},{... | collective-permute-start | bytes 172040 | tf_op jit(solution)/shard_map/ppermute | solution.py:261
  60.3 7.1 %collective-permute-start.15 = (bf16[16,1792]{1,0:T(8,128)(2,1)S(1)}, bf16[16,1792]{1,0:T(8,128)(2,1)S(1)}, u32[]{:S(2)}, u32[]{:S(2)}) collective-permute-start(bf16[16,1792]{1,0:T(8,128)(2,1)S(1)} %get-tuple-element.163), channel_id=1, source_target_pairs={{0,128},{8,136},{16,144},{24,152},{32,160},{40,168},{48,176},{56,1... | collective-permute-start | bytes 172040 | tf_op jit(solution)/shard_map/ppermute | solution.py:261
  61.4 6.1 %collective-permute-start.14 = (bf16[16,1792]{1,0:T(8,128)(2,1)S(1)}, bf16[16,1792]{1,0:T(8,128)(2,1)S(1)}, u32[]{:S(2)}, u32[]{:S(2)}) collective-permute-start(bf16[16,1792]{1,0:T(8,128)(2,1)S(1)} %get-tuple-element.163), channel_id=1, source_target_pairs={{0,192},{8,200},{16,208},{24,216},{32,224},{40,232},{48,240},{56,2... | collective-permute-start | bytes 172040 | tf_op jit(solution)/shard_map/ppermute | solution.py:261
  64.2 7.5 %collective-permute-start.11 = (bf16[80,1280]{1,0:T(8,128)(2,1)S(1)}, bf16[80,1280]{1,0:T(8,128)(2,1)S(1)}, u32[]{:S(2)}, u32[]{:S(2)}) collective-permute-start(bf16[80,1280]{1,0:T(8,128)(2,1)S(1)} %get-tuple-element.90), channel_id=1, source_target_pairs={{0,1},{1,2},{2,3},{3,0},{4,5},{5,6},{6,7},{7,4},{8,9},{9,10},{10,1... | collective-permute-start | bytes 614408 | tf_op jit(solution)/shard_map/ppermute | solution.py:251
  64.2 7.5 %collective-permute-start.12 = (bf16[80,1280]{1,0:T(8,128)(2,1)S(1)}, bf16[80,1280]{1,0:T(8,128)(2,1)S(1)}, u32[]{:S(2)}, u32[]{:S(2)}) collective-permute-start(bf16[80,1280]{1,0:T(8,128)(2,1)S(1)} %get-tuple-element.91), channel_id=1, source_target_pairs={{0,3},{1,0},{2,1},{3,2},{4,7},{5,4},{6,5},{7,6},{8,11},{9,8},{10,9... | collective-permute-start | bytes 614408 | tf_op jit(solution)/shard_map/ppermute | solution.py:251
  71.9 14.7 %collective-permute-start.16 = (bf16[160,1280]{1,0:T(8,128)(2,1)S(1)}, bf16[160,1280]{1,0:T(8,128)(2,1)S(1)}, u32[]{:S(2)}, u32[]{:S(2)}) collective-permute-start(bf16[160,1280]{1,0:T(8,128)(2,1)S(1)} %get-tuple-element.96), channel_id=1, source_target_pairs={{0,1},{1,2},{2,3},{3,0},{4,5},{5,6},{6,7},{7,4},{8,9},{9,10},{10,1... | collective-permute-start | bytes 1228808 | tf_op jit(solution)/shard_map/ppermute | solution.py:251
  72.0 14.6 %collective-permute-start.17 = (bf16[160,1280]{1,0:T(8,128)(2,1)S(1)}, bf16[160,1280]{1,0:T(8,128)(2,1)S(1)}, u32[]{:S(2)}, u32[]{:S(2)}) collective-permute-start(bf16[160,1280]{1,0:T(8,128)(2,1)S(1)} %get-tuple-element.97), channel_id=1, source_target_pairs={{0,3},{1,0},{2,1},{3,2},{4,7},{5,4},{6,5},{7,6},{8,11},{9,8},{10,9... | collective-permute-start | bytes 1228808 | tf_op jit(solution)/shard_map/ppermute | solution.py:251
  75.5 8.8 %collective-permute-start.3 = (bf16[80,1280]{1,0:T(8,128)(2,1)S(1)}, bf16[80,1280]{1,0:T(8,128)(2,1)S(1)}, u32[]{:S(2)}, u32[]{:S(2)}) collective-permute-start(bf16[80,1280]{1,0:T(8,128)(2,1)S(1)} %get-tuple-element.83), channel_id=1, source_target_pairs={{0,1},{1,2},{2,3},{3,0},{4,5},{5,6},{6,7},{7,4},{8,9},{9,10},{10,1... | collective-permute-start | bytes 614408 | tf_op jit(solution)/shard_map/ppermute | solution.py:251
  75.5 9.3 %collective-permute-start.4 = (bf16[80,1280]{1,0:T(8,128)(2,1)S(1)}, bf16[80,1280]{1,0:T(8,128)(2,1)S(1)}, u32[]{:S(2)}, u32[]{:S(2)}) collective-permute-start(bf16[80,1280]{1,0:T(8,128)(2,1)S(1)} %get-tuple-element.84), channel_id=1, source_target_pairs={{0,3},{1,0},{2,1},{3,2},{4,7},{5,4},{6,5},{7,6},{8,11},{9,8},{10,9... | collective-permute-start | bytes 614408 | tf_op jit(solution)/shard_map/ppermute | solution.py:251
  78.7 13.8 %collective-permute-start.21 = (bf16[64,1792]{1,0:T(8,128)(2,1)S(1)}, bf16[64,1792]{1,0:T(8,128)(2,1)S(1)}, u32[]{:S(2)}, u32[]{:S(2)}) collective-permute-start(bf16[64,1792]{1,0:T(8,128)(2,1)S(1)} %constant_dynamic-update-slice_fusion.2), channel_id=1, source_target_pairs={{0,32},{8,40},{16,48},{24,56},{32,0},{40,8},{48,16},{56,24},{64,96... | collective-permute-start | bytes 688136 | tf_op jit(solution)/shard_map/ppermute | solution.py:261
  84.3 10.9 %collective-permute-start.20 = (bf16[64,1792]{1,0:T(8,128)(2,1)S(1)}, bf16[64,1792]{1,0:T(8,128)(2,1)S(1)}, u32[]{:S(2)}, u32[]{:S(2)}) collective-permute-start(bf16[64,1792]{1,0:T(8,128)(2,1)S(1)} %constant_dynamic-update-slice_fusion.2), channel_id=1, source_target_pairs={{0,48},{8,56},{16,0},{24,8},{32,16},{40,24},{48,32},{56,40},{64,11... | collective-permute-start | bytes 688136 | tf_op jit(solution)/shard_map/ppermute | solution.py:261
  84.8 10.4 %collective-permute-start.19 = (bf16[64,1792]{1,0:T(8,128)(2,1)S(1)}, bf16[64,1792]{1,0:T(8,128)(2,1)S(1)}, u32[]{:S(2)}, u32[]{:S(2)}) collective-permute-start(bf16[64,1792]{1,0:T(8,128)(2,1)S(1)} %constant_dynamic-update-slice_fusion.2), channel_id=1, source_target_pairs={{0,16},{8,24},{16,32},{24,40},{32,48},{40,56},{48,0},{56,8},{64,80... | collective-permute-start | bytes 688136 | tf_op jit(solution)/shard_map/ppermute | solution.py:261
  86.5 14.9 %copy-start.9 = (s32[2]{0:T(128)S(1)}, s32[2]{0:T(128)}, u32[]{:S(2)}) copy-start(s32[2]{0:T(128)} %length_ref.3) | copy-start | bytes 28
  86.7 14.8 %collective-permute-start.18 = (bf16[160,1280]{1,0:T(8,128)(2,1)S(1)}, bf16[160,1280]{1,0:T(8,128)(2,1)S(1)}, u32[]{:S(2)}, u32[]{:S(2)}) collective-permute-start(bf16[160,1280]{1,0:T(8,128)(2,1)S(1)} %shard_map.144), channel_id=1, source_target_pairs={{0,4},{1,5},{2,6},{3,7},{4,0},{5,1},{6,2},{7,3},{8,12},{9,13},{10,... | collective-permute-start | bytes 1228808 | tf_op jit(solution)/shard_map/ppermute | solution.py:251
  92.0 9.5 %collective-permute-start.5 = (bf16[160,1280]{1,0:T(8,128)(2,1)S(1)}, bf16[160,1280]{1,0:T(8,128)(2,1)S(1)}, u32[]{:S(2)}, u32[]{:S(2)}) collective-permute-start(bf16[160,1280]{1,0:T(8,128)(2,1)S(1)} %get-tuple-element.85), channel_id=1, source_target_pairs={{0,1},{1,2},{2,3},{3,0},{4,5},{5,6},{6,7},{7,4},{8,9},{9,10},{10,1... | collective-permute-start | bytes 1228808 | tf_op jit(solution)/shard_map/ppermute | solution.py:251
  92.5 8.9 %collective-permute-start.6 = (bf16[160,1280]{1,0:T(8,128)(2,1)S(1)}, bf16[160,1280]{1,0:T(8,128)(2,1)S(1)}, u32[]{:S(2)}, u32[]{:S(2)}) collective-permute-start(bf16[160,1280]{1,0:T(8,128)(2,1)S(1)} %get-tuple-element.86), channel_id=1, source_target_pairs={{0,3},{1,0},{2,1},{3,2},{4,7},{5,4},{6,5},{7,6},{8,11},{9,8},{10,9... | collective-permute-start | bytes 1228808 | tf_op jit(solution)/shard_map/ppermute | solution.py:251
  104.0 20.0 %collective-permute-start.28 = (bf16[256,1792]{1,0:T(8,128)(2,1)}, bf16[256,1792]{1,0:T(8,128)(2,1)}, u32[]{:S(2)}, u32[]{:S(2)}) collective-permute-start(bf16[256,1792]{1,0:T(8,128)(2,1)} %pad_maximum_fusion.1), channel_id=1, source_target_pairs={{0,8},{8,0},{16,24},{24,16},{32,40},{40,32},{48,56},{56,48},{64,72... | collective-permute-start | bytes 2752520 | tf_op jit(solution)/shard_map/ppermute | solution.py:261
  104.0 16.3 %collective-permute-start.24 = (bf16[2,1280]{1,0:T(2,128)(2,1)S(1)}, bf16[2,1280]{1,0:T(2,128)(2,1)S(1)}, u32[]{:S(2)}, u32[]{:S(2)}) collective-permute-start(bf16[2,1280]{1,0:T(2,128)(2,1)S(1)} %get-tuple-element.105), channel_id=1, source_target_pairs={{0,2},{1,3},{2,0},{3,1},{4,6},{5,7},{6,4},{7,5},{8,10},{9,11},{10,... | collective-permute-start | bytes 15368 | tf_op jit(solution)/shard_map/ppermute | solution.py:251
  106.7 13.6 %collective-permute-start.23 = (bf16[2,1280]{1,0:T(2,128)(2,1)S(1)}, bf16[2,1280]{1,0:T(2,128)(2,1)S(1)}, u32[]{:S(2)}, u32[]{:S(2)}) collective-permute-start(bf16[2,1280]{1,0:T(2,128)(2,1)S(1)} %get-tuple-element.105), channel_id=1, source_target_pairs={{0,3},{1,0},{2,1},{3,2},{4,7},{5,4},{6,5},{7,6},{8,11},{9,8},{10,9... | collective-permute-start | bytes 15368 | tf_op jit(solution)/shard_map/ppermute | solution.py:251
  116.3 7.7 %collective-permute-start.22 = (bf16[2,1280]{1,0:T(2,128)(2,1)S(1)}, bf16[2,1280]{1,0:T(2,128)(2,1)S(1)}, u32[]{:S(2)}, u32[]{:S(2)}) collective-permute-start(bf16[2,1280]{1,0:T(2,128)(2,1)S(1)} %get-tuple-element.105), channel_id=1, source_target_pairs={{0,1},{1,2},{2,3},{3,0},{4,5},{5,6},{6,7},{7,4},{8,9},{9,10},{10,1... | collective-permute-start | bytes 15368 | tf_op jit(solution)/shard_map/ppermute | solution.py:251
  118.0 13.0 %collective-permute-start.26 = (bf16[160,1280]{1,0:T(8,128)(2,1)}, bf16[160,1280]{1,0:T(8,128)(2,1)S(1)}, u32[]{:S(2)}, u32[]{:S(2)}) collective-permute-start(bf16[160,1280]{1,0:T(8,128)(2,1)} %copy-done.15), channel_id=1, source_target_pairs={{0,3},{1,0},{2,1},{3,2},{4,7},{5,4},{6,5},{7,6},{8,11},{9,8},{10,9... | collective-permute-start | bytes 1228808 | tf_op jit(solution)/shard_map/ppermute | solution.py:251
  120.3 12.2 %collective-permute-start.25 = (bf16[160,1280]{1,0:T(8,128)(2,1)}, bf16[160,1280]{1,0:T(8,128)(2,1)S(1)}, u32[]{:S(2)}, u32[]{:S(2)}) collective-permute-start(bf16[160,1280]{1,0:T(8,128)(2,1)} %copy-done.15), channel_id=1, source_target_pairs={{0,1},{1,2},{2,3},{3,0},{4,5},{5,6},{6,7},{7,4},{8,9},{9,10},{10,1... | collective-permute-start | bytes 1228808 | tf_op jit(solution)/shard_map/ppermute | solution.py:251
  120.3 10.7 %collective-permute-start.27 = (bf16[80,1280]{1,0:T(8,128)(2,1)}, bf16[80,1280]{1,0:T(8,128)(2,1)S(1)}, u32[]{:S(2)}, u32[]{:S(2)}) collective-permute-start(bf16[80,1280]{1,0:T(8,128)(2,1)} %copy-done.17), channel_id=1, source_target_pairs={{0,4},{1,5},{2,6},{3,7},{4,0},{5,1},{6,2},{7,3},{8,12},{9,13},{10,... | collective-permute-start | bytes 614408 | tf_op jit(solution)/shard_map/ppermute | solution.py:251
  134.0 10.9 %copy-start.32 = (bf16[512,1664]{1,0:T(8,128)(2,1)}, bf16[512,1664]{1,0:T(8,128)(2,1)S(1)}, u32[]{:S(2)}) copy-start(bf16[512,1664]{1,0:T(8,128)(2,1)S(1)} %fusion.4) | copy-start | bytes 5111812
  134.0 10.9 %collective-permute-start.29 = (bf16[8,1280]{1,0:T(8,128)(2,1)S(1)}, bf16[8,1280]{1,0:T(8,128)(2,1)S(1)}, u32[]{:S(2)}, u32[]{:S(2)}) collective-permute-start(bf16[8,1280]{1,0:T(8,128)(2,1)S(1)} %pad_maximum_fusion.6), channel_id=1, source_target_pairs={{0,4},{1,5},{2,6},{3,7},{4,0},{5,1},{6,2},{7,3},{8,12},{9,13},{10,... | collective-permute-start | bytes 61448 | tf_op jit(solution)/shard_map/ppermute | solution.py:251
  137.9 9.9 %collective-permute-start.31 = (bf16[80,1280]{1,0:T(8,128)(2,1)S(1)}, bf16[80,1280]{1,0:T(8,128)(2,1)S(1)}, u32[]{:S(2)}, u32[]{:S(2)}) collective-permute-start(bf16[80,1280]{1,0:T(8,128)(2,1)S(1)} %get-tuple-element.114), channel_id=1, source_target_pairs={{0,4},{1,5},{2,6},{3,7},{4,0},{5,1},{6,2},{7,3},{8,12},{9,13},{10,... | collective-permute-start | bytes 614408 | tf_op jit(solution)/shard_map/ppermute | solution.py:251
  140.0 10.5 %collective-permute-start.30 = (bf16[160,1280]{1,0:T(8,128)(2,1)S(1)}, bf16[160,1280]{1,0:T(8,128)(2,1)S(1)}, u32[]{:S(2)}, u32[]{:S(2)}) collective-permute-start(bf16[160,1280]{1,0:T(8,128)(2,1)S(1)} %collective-permute-done.25.h1), channel_id=1, source_target_pairs={{0,1},{1,2},{2,3},{3,0},{4,5},{5,6},{6,7},{7,4},{8,9},{9,10},{10,1... | collective-permute-start | bytes 1228808 | tf_op jit(solution)/shard_map/ppermute | solution.py:251
  144.9 39.5 %copy-start.30 = (f32[512,1280]{1,0:T(8,128)}, f32[512,1280]{1,0:T(8,128)S(1)}, u32[]{:S(2)}) copy-start(f32[512,1280]{1,0:T(8,128)S(1)} %get-tuple-element.170) | copy-start | bytes 7864324
  150.5 10.8 %collective-permute-start.34 = (bf16[16,1280]{1,0:T(8,128)(2,1)S(1)}, bf16[16,1280]{1,0:T(8,128)(2,1)S(1)}, u32[]{:S(2)}, u32[]{:S(2)}) collective-permute-start(bf16[16,1280]{1,0:T(8,128)(2,1)S(1)} %pad_maximum_fusion.5), channel_id=1, source_target_pairs={{0,128},{8,136},{16,144},{24,152},{32,160},{40,168},{48,176},{56,1... | collective-permute-start | bytes 122888 | tf_op jit(solution)/shard_map/ppermute | solution.py:261
  157.2 4.3 %collective-permute-start.33 = (bf16[16,1280]{1,0:T(8,128)(2,1)S(1)}, bf16[16,1280]{1,0:T(8,128)(2,1)S(1)}, u32[]{:S(2)}, u32[]{:S(2)}) collective-permute-start(bf16[16,1280]{1,0:T(8,128)(2,1)S(1)} %pad_maximum_fusion.5), channel_id=1, source_target_pairs={{0,192},{8,200},{16,208},{24,216},{32,224},{40,232},{48,240},{56,2... | collective-permute-start | bytes 122888 | tf_op jit(solution)/shard_map/ppermute | solution.py:261
  157.8 5.8 %collective-permute-start.32 = (bf16[16,1280]{1,0:T(8,128)(2,1)S(1)}, bf16[16,1280]{1,0:T(8,128)(2,1)S(1)}, u32[]{:S(2)}, u32[]{:S(2)}) collective-permute-start(bf16[16,1280]{1,0:T(8,128)(2,1)S(1)} %pad_maximum_fusion.5), channel_id=1, source_target_pairs={{0,64},{8,72},{16,80},{24,88},{32,96},{40,104},{48,112},{56,120},{... | collective-permute-start | bytes 122888 | tf_op jit(solution)/shard_map/ppermute | solution.py:261
  159.2 9.1 %collective-permute-start.36 = (bf16[160,1280]{1,0:T(8,128)(2,1)S(1)}, bf16[160,1280]{1,0:T(8,128)(2,1)S(1)}, u32[]{:S(2)}, u32[]{:S(2)}) collective-permute-start(bf16[160,1280]{1,0:T(8,128)(2,1)S(1)} %pad_maximum_fusion.3.h4), channel_id=1, source_target_pairs={{0,3},{1,0},{2,1},{3,2},{4,7},{5,4},{6,5},{7,6},{8,11},{9,8},{10,9... | collective-permute-start | bytes 1228808 | tf_op jit(solution)/shard_map/ppermute | solution.py:251
  160.9 10.0 %collective-permute-start.35 = (bf16[160,1280]{1,0:T(8,128)(2,1)S(1)}, bf16[160,1280]{1,0:T(8,128)(2,1)S(1)}, u32[]{:S(2)}, u32[]{:S(2)}) collective-permute-start(bf16[160,1280]{1,0:T(8,128)(2,1)S(1)} %pad_maximum_fusion.3.h4), channel_id=1, source_target_pairs={{0,1},{1,2},{2,3},{3,0},{4,5},{5,6},{6,7},{7,4},{8,9},{9,10},{10,1... | collective-permute-start | bytes 1228808 | tf_op jit(solution)/shard_map/ppermute | solution.py:251
  170.9 7.2 %collective-permute-start.39 = (bf16[64,1280]{1,0:T(8,128)(2,1)S(1)}, bf16[64,1280]{1,0:T(8,128)(2,1)S(1)}, u32[]{:S(2)}, u32[]{:S(2)}) collective-permute-start(bf16[64,1280]{1,0:T(8,128)(2,1)S(1)} %pad_maximum_fusion.4), channel_id=1, source_target_pairs={{0,32},{8,40},{16,48},{24,56},{32,0},{40,8},{48,16},{56,24},{64,96... | collective-permute-start | bytes 491528 | tf_op jit(solution)/shard_map/ppermute | solution.py:261
  174.2 5.6 %collective-permute-start.38 = (bf16[64,1280]{1,0:T(8,128)(2,1)S(1)}, bf16[64,1280]{1,0:T(8,128)(2,1)S(1)}, u32[]{:S(2)}, u32[]{:S(2)}) collective-permute-start(bf16[64,1280]{1,0:T(8,128)(2,1)S(1)} %pad_maximum_fusion.4), channel_id=1, source_target_pairs={{0,48},{8,56},{16,0},{24,8},{32,16},{40,24},{48,32},{56,40},{64,11... | collective-permute-start | bytes 491528 | tf_op jit(solution)/shard_map/ppermute | solution.py:261
  174.6 5.3 %collective-permute-start.37 = (bf16[64,1280]{1,0:T(8,128)(2,1)S(1)}, bf16[64,1280]{1,0:T(8,128)(2,1)S(1)}, u32[]{:S(2)}, u32[]{:S(2)}) collective-permute-start(bf16[64,1280]{1,0:T(8,128)(2,1)S(1)} %pad_maximum_fusion.4), channel_id=1, source_target_pairs={{0,16},{8,24},{16,32},{24,40},{32,48},{40,56},{48,0},{56,8},{64,80... | collective-permute-start | bytes 491528 | tf_op jit(solution)/shard_map/ppermute | solution.py:261
  176.3 8.0 %collective-permute-start.40 = (bf16[160,1280]{1,0:T(8,128)(2,1)S(1)}, bf16[160,1280]{1,0:T(8,128)(2,1)S(1)}, u32[]{:S(2)}, u32[]{:S(2)}) collective-permute-start(bf16[160,1280]{1,0:T(8,128)(2,1)S(1)} %collective-permute-done.36.h6), channel_id=1, source_target_pairs={{0,3},{1,0},{2,1},{3,2},{4,7},{5,4},{6,5},{7,6},{8,11},{9,8},{10,9... | collective-permute-start | bytes 1228808 | tf_op jit(solution)/shard_map/ppermute | solution.py:251
  184.2 2.1 collective-permute-start.41
  193.4 9.3 %copy-start.29 = (bf16[640,640]{1,0:T(8,128)(2,1)S(1)}, bf16[640,640]{1,0:T(8,128)(2,1)}, u32[]{:S(2)}) copy-start(bf16[640,640]{1,0:T(8,128)(2,1)} %copy-done.28) | copy-start | bytes 2457604
  208.3 3.2 %collective-permute-start.42 = (bf16[640,640]{1,0:T(8,128)(2,1)S(1)}, bf16[640,640]{1,0:T(8,128)(2,1)S(1)}, u32[]{:S(2)}, u32[]{:S(2)}) collective-permute-start(bf16[640,640]{1,0:T(8,128)(2,1)S(1)} %get-tuple-element.138), channel_id=1, source_target_pairs={{0,8},{8,0},{16,24},{24,16},{32,40},{40,32},{48,56},{56,48},{64,72... | collective-permute-start | bytes 2457608 | tf_op jit(solution)/shard_map/ppermute | solution.py:261
  209.3 8.1 %collective-permute-start.49 = (bf16[640,640]{1,0:T(8,128)(2,1)S(1)}, bf16[640,640]{1,0:T(8,128)(2,1)S(1)}, u32[]{:S(2)}, u32[]{:S(2)}) collective-permute-start(bf16[640,640]{1,0:T(8,128)(2,1)S(1)} %get-tuple-element.148), channel_id=1, source_target_pairs={{0,8},{8,0},{16,24},{24,16},{32,40},{40,32},{48,56},{56,48},{64,72... | collective-permute-start | bytes 2457608 | tf_op jit(solution)/shard_map/ppermute | solution.py:261
  212.7 8.6 %collective-permute-start.43 = (bf16[160,640]{1,0:T(8,128)(2,1)S(1)}, bf16[160,640]{1,0:T(8,128)(2,1)S(1)}, u32[]{:S(2)}, u32[]{:S(2)}) collective-permute-start(bf16[160,640]{1,0:T(8,128)(2,1)S(1)} %get-tuple-element.140), channel_id=1, source_target_pairs={{0,16},{8,24},{16,32},{24,40},{32,48},{40,56},{48,0},{56,8},{64,80... | collective-permute-start | bytes 614408 | tf_op jit(solution)/shard_map/ppermute | solution.py:261
  213.6 14.1 %collective-permute-start.44 = (bf16[160,640]{1,0:T(8,128)(2,1)}, bf16[160,640]{1,0:T(8,128)(2,1)}, u32[]{:S(2)}, u32[]{:S(2)}) collective-permute-start(bf16[160,640]{1,0:T(8,128)(2,1)} %get-tuple-element.141), channel_id=1, source_target_pairs={{0,48},{8,56},{16,0},{24,8},{32,16},{40,24},{48,32},{56,40},{64,11... | collective-permute-start | bytes 614408 | tf_op jit(solution)/shard_map/ppermute | solution.py:261
  215.6 12.4 %collective-permute-start.45 = (bf16[160,640]{1,0:T(8,128)(2,1)}, bf16[160,640]{1,0:T(8,128)(2,1)}, u32[]{:S(2)}, u32[]{:S(2)}) collective-permute-start(bf16[160,640]{1,0:T(8,128)(2,1)} %get-tuple-element.142), channel_id=1, source_target_pairs={{0,32},{8,40},{16,48},{24,56},{32,0},{40,8},{48,16},{56,24},{64,96... | collective-permute-start | bytes 614408 | tf_op jit(solution)/shard_map/ppermute | solution.py:261
  219.3 15.8 %collective-permute-start.50 = (bf16[160,640]{1,0:T(8,128)(2,1)}, bf16[160,640]{1,0:T(8,128)(2,1)S(1)}, u32[]{:S(2)}, u32[]{:S(2)}) collective-permute-start(bf16[160,640]{1,0:T(8,128)(2,1)} %get-tuple-element.150), channel_id=1, source_target_pairs={{0,16},{8,24},{16,32},{24,40},{32,48},{40,56},{48,0},{56,8},{64,80... | collective-permute-start | bytes 614408 | tf_op jit(solution)/shard_map/ppermute | solution.py:261
  220.6 16.0 %collective-permute-start.51 = (bf16[160,640]{1,0:T(8,128)(2,1)}, bf16[160,640]{1,0:T(8,128)(2,1)}, u32[]{:S(2)}, u32[]{:S(2)}) collective-permute-start(bf16[160,640]{1,0:T(8,128)(2,1)} %get-tuple-element.151), channel_id=1, source_target_pairs={{0,48},{8,56},{16,0},{24,8},{32,16},{40,24},{48,32},{56,40},{64,11... | collective-permute-start | bytes 614408 | tf_op jit(solution)/shard_map/ppermute | solution.py:261
  222.0 14.6 %collective-permute-start.52 = (bf16[160,640]{1,0:T(8,128)(2,1)}, bf16[160,640]{1,0:T(8,128)(2,1)}, u32[]{:S(2)}, u32[]{:S(2)}) collective-permute-start(bf16[160,640]{1,0:T(8,128)(2,1)} %get-tuple-element.152), channel_id=1, source_target_pairs={{0,32},{8,40},{16,48},{24,56},{32,0},{40,8},{48,16},{56,24},{64,96... | collective-permute-start | bytes 614408 | tf_op jit(solution)/shard_map/ppermute | solution.py:261
  231.1 11.5 %collective-permute-start.46 = (bf16[40,640]{1,0:T(8,128)(2,1)S(1)}, bf16[40,640]{1,0:T(8,128)(2,1)S(1)}, u32[]{:S(2)}, u32[]{:S(2)}) collective-permute-start(bf16[40,640]{1,0:T(8,128)(2,1)S(1)} %get-tuple-element.144), channel_id=1, source_target_pairs={{0,64},{8,72},{16,80},{24,88},{32,96},{40,104},{48,112},{56,120},{... | collective-permute-start | bytes 153608 | tf_op jit(solution)/shard_map/ppermute | solution.py:261
  232.3 11.5 %collective-permute-start.47 = (bf16[40,640]{1,0:T(8,128)(2,1)S(1)}, bf16[40,640]{1,0:T(8,128)(2,1)S(1)}, u32[]{:S(2)}, u32[]{:S(2)}) collective-permute-start(bf16[40,640]{1,0:T(8,128)(2,1)S(1)} %get-tuple-element.145), channel_id=1, source_target_pairs={{0,192},{8,200},{16,208},{24,216},{32,224},{40,232},{48,240},{56,2... | collective-permute-start | bytes 153608 | tf_op jit(solution)/shard_map/ppermute | solution.py:261
  235.1 8.8 %collective-permute-start.48 = (bf16[40,640]{1,0:T(8,128)(2,1)S(1)}, bf16[40,640]{1,0:T(8,128)(2,1)S(1)}, u32[]{:S(2)}, u32[]{:S(2)}) collective-permute-start(bf16[40,640]{1,0:T(8,128)(2,1)S(1)} %get-tuple-element.146), channel_id=1, source_target_pairs={{0,128},{8,136},{16,144},{24,152},{32,160},{40,168},{48,176},{56,1... | collective-permute-start | bytes 153608 | tf_op jit(solution)/shard_map/ppermute | solution.py:261
  238.8 6.1 %collective-permute-start.53 = (bf16[40,640]{1,0:T(8,128)(2,1)S(1)}, bf16[40,640]{1,0:T(8,128)(2,1)S(1)}, u32[]{:S(2)}, u32[]{:S(2)}) collective-permute-start(bf16[40,640]{1,0:T(8,128)(2,1)S(1)} %get-tuple-element.154), channel_id=1, source_target_pairs={{0,64},{8,72},{16,80},{24,88},{32,96},{40,104},{48,112},{56,120},{... | collective-permute-start | bytes 153608 | tf_op jit(solution)/shard_map/ppermute | solution.py:261
  240.2 5.1 %collective-permute-start.54 = (bf16[40,640]{1,0:T(8,128)(2,1)S(1)}, bf16[40,640]{1,0:T(8,128)(2,1)S(1)}, u32[]{:S(2)}, u32[]{:S(2)}) collective-permute-start(bf16[40,640]{1,0:T(8,128)(2,1)S(1)} %get-tuple-element.155), channel_id=1, source_target_pairs={{0,192},{8,200},{16,208},{24,216},{32,224},{40,232},{48,240},{56,2... | collective-permute-start | bytes 153608 | tf_op jit(solution)/shard_map/ppermute | solution.py:261
  242.7 5.0 %collective-permute-start.55 = (bf16[40,640]{1,0:T(8,128)(2,1)S(1)}, bf16[40,640]{1,0:T(8,128)(2,1)S(1)}, u32[]{:S(2)}, u32[]{:S(2)}) collective-permute-start(bf16[40,640]{1,0:T(8,128)(2,1)S(1)} %get-tuple-element.156), channel_id=1, source_target_pairs={{0,128},{8,136},{16,144},{24,152},{32,160},{40,168},{48,176},{56,1... | collective-permute-start | bytes 153608 | tf_op jit(solution)/shard_map/ppermute | solution.py:261
  (29 other events, 93.6 us)
